TPU v7x, 512 devices: a whole 4x4x16 slice. The times are simulated.
512 devices in a mesh: tm: 128 (over y, x, z_lo), head: 4 (over z_hi, core).
Axes of the slice: x: 4, y: 4, z: 16 (z_hi: 2, z_lo: 8; z = z_hi * 8 + z_lo), core: 2. Of those that a mesh axis runs over, the one named last changes fastest.
Arguments:
- latent: bfloat16 [128, 256, 1920], P('tm', None, 'head'), may hold values from -6 to 6
- start_frame: int32 [128], P('tm'), may hold values from 0 to 1
- norm_gains: float32 [2, 1920], replicated, may hold values from 0.1 to 1.9
- qkv_weight: bfloat16 [2, 1920, 3, 1024], P(None, 'tm', None, 'head')
- out_weight: bfloat16 [2, 1024, 1920], P(None, 'head', 'tm'), may hold values from -0.75 to 0.75
Outputs:
- refined: bfloat16 [128, 256, 1920], P('head', 'tm')
All inputs are finite; a program needn't handle non-finite values.
Results may differ from a plain program's by a relative error of at most 0.035.
Values may be sent and summed in bfloat16 or wider, within the bound.
A program may use at most 64 MiB of HBM per device.

v0:
```python
import jax
import jax.numpy as jnp
from jax import lax
from jax.sharding import PartitionSpec as P

HEAD_DIM = 64
LAYERS = 2
CLIP_STRETCHES = 8
STRETCH_FRAMES = 2


EPSILON = 1e-06


def shifted(value, axis, steps):
    count = lax.axis_size(axis)
    initial, last = (max(0, -steps), min(count, count - steps))
    return lax.ppermute(value, axis, [(source, source + steps) for source in range(initial, last)])


def attend(queries, key_rows, value_rows, prev_keys, prev_values, visible, head_dim):
    row_count = queries.shape[0]
    head_count = queries.shape[1] // head_dim
    shaped = (row_count, head_count, head_dim)
    factor = head_dim ** (-0.5)
    query_b = queries.reshape(shaped)
    own_scores = (
        jnp.einsum(
            "qhd,khd->hqk", query_b, key_rows.reshape(shaped), preferred_element_type=jnp.float32
        )
        * factor
    )
    past_scores = (
        jnp.einsum(
            "qhd,khd->hqk", query_b, prev_keys.reshape(shaped), preferred_element_type=jnp.float32
        )
        * factor
    )
    past_scores = jnp.where(visible[None, None, :], past_scores, -jnp.inf)
    scores = jnp.concatenate([own_scores, past_scores], axis=2)
    highest = jnp.max(scores, axis=2, keepdims=True)
    exponent = jnp.exp(scores - highest)
    weights = (exponent / jnp.sum(exponent, axis=2, keepdims=True)).astype(jnp.bfloat16)
    both_values = jnp.concatenate([value_rows, prev_values], axis=0).reshape(
        2 * row_count, head_count, head_dim
    )
    blended = jnp.einsum("hqk,khd->qhd", weights, both_values, preferred_element_type=jnp.float32)
    return blended.astype(jnp.bfloat16).reshape(row_count, head_count * head_dim)


def local(latent, start_frame, norm_gains, qkv_weight, out_weight):
    resident = lax.all_to_all(
        lax.all_to_all(latent, "tm", split_axis=1, concat_axis=0, tiled=True),
        "head",
        split_axis=0,
        concat_axis=2,
        tiled=True,
    ).astype(jnp.float32)
    boundary = start_frame[0]
    clip_start = lax.axis_index("tm") % CLIP_STRETCHES == 0
    for layer_num in range(LAYERS):
        mean_square = jnp.mean(resident * resident, axis=-1, keepdims=True)
        normed = (resident * lax.rsqrt(mean_square + EPSILON) * norm_gains[layer_num]).astype(
            jnp.bfloat16
        )
        gathered = lax.all_gather(normed, "head", axis=0, tiled=True)
        stretch_rows = gathered.reshape(-1, gathered.shape[2])
        row_count = stretch_rows.shape[0]
        layer_qkv, layer_out = (
            lax.all_gather(qkv_weight[layer_num], "tm", axis=0, tiled=True),
            lax.all_gather(out_weight[layer_num], "tm", axis=1, tiled=True),
        )
        projected = jnp.einsum(
            "rd,dcj->rcj", stretch_rows, layer_qkv, preferred_element_type=jnp.float32
        ).astype(jnp.bfloat16)
        queries = projected[:, 0]
        key_rows = projected[:, 1]
        value_rows = projected[:, 2]
        prev_keys, prev_values = shifted((key_rows, value_rows), "tm", 1)
        frame_of = jnp.arange(row_count) % STRETCH_FRAMES
        visible = (frame_of >= boundary) & jnp.logical_not(clip_start)
        blended = attend(queries, key_rows, value_rows, prev_keys, prev_values, visible, HEAD_DIM)
        partial_out = jnp.dot(blended, layer_out, preferred_element_type=jnp.float32)
        summed = lax.psum_scatter(
            partial_out.reshape(gathered.shape).astype(jnp.bfloat16),
            "head",
            scatter_dimension=0,
            tiled=True,
        ).astype(jnp.float32)
        resident = resident + summed
    return resident.astype(jnp.bfloat16)


def solution(mesh):
    return jax.shard_map(
        local,
        mesh=mesh,
        in_specs=(
            P("tm", None, "head"),
            P("tm"),
            P(),
            P(None, "tm", None, "head"),
            P(None, "head", "tm"),
        ),
        out_specs=P("head", "tm", None),
        check_vma=False,
    )
```

profile of v0, /device:TPU:1, one launch (start us, length us, event | category | flops | bytes accessed | tf_op | source)
XLA Modules:
  0.0 2149.1 jit_solution(18306985354880431436)
XLA Ops:
  8.9 1.3 copy.108
  10.8 2.3 reduce.14
  13.2 42.4 %all_to_all.21 = bf16[128,2,480]{2,1,0:T(2,128)(2,1)S(1)} all-to-all(bf16[128,2,480]{2,1,0:T(2,128)(2,1)S(1)} %reshape.98), channel_id=1, replica_groups=mesh['tm'=128,'head'=4] {'tm'}, dimensions={0} | all-to-all | bytes 491520 | tf_op jit(solution)/shard_map/all_to_all | solution.py:53
  55.9 1.5 bitcast_reduce_fusion
  58.1 8.4 all-to-all-start.1
  67.2 487.2 %all-gather.1 = bf16[1,256,1920]{1,0,2:T(2,128)(2,1)S(1)} all-gather(bf16[1,256,15]{1,0,2:T(2,128)(2,1)S(1)} %get-tuple-element.19), channel_id=3, replica_groups=mesh['tm'=128,'head'=4] {'tm'}, dimensions={2}, use_global_device_ids=true | all-gather | bytes 990720 | tf_op jit(solution)/shard_map/all_gather | solution.py:71
  554.5 2.5 copy.119
  558.7 73.9 %all_gather.18 = bf16[128,2,1920]{2,0,1:T(8,128)(2,1)S(1)} all-gather(bf16[32,2,1920]{2,0,1:T(8,128)(2,1)S(1)} %multiply_convert_fusion.1), channel_id=1, replica_groups=mesh['tm'=128,'head'=4] {'head'}, dimensions={0}, use_global_device_ids=true | all-gather | bytes 1228800 | tf_op jit(solution)/shard_map/all_gather | solution.py:66
  632.6 1.0 copy.114
  634.0 268.4 %all-gather.7.cloned.1.call-done = bf16[1,1920,3,256]{3,2,0,1:T(4,128)(2,1)} async-done(((bf16[1,15,3,256]{3,2,0,1:T(4,128)(2,1)}), bf16[1,1920,3,256]{3,2,0,1:T(4,128)(2,1)}) %all-gather.7.cloned.1.call-update) | async-done | bytes 2949136 | tf_op jit(solution)/shard_map/all_gather | solution.py:70
  902.4 7.2 copy.116
  909.6 2.8 fusion.10
  912.5 1.3 collective-permute-start.1
  913.8 1.5 collective-permute-start
  918.0 1.4 convolution_convert_fusion.1
  919.4 491.2 %all-gather.3 = bf16[1,256,1920]{1,0,2:T(2,128)(2,1)S(1)} all-gather(bf16[1,256,15]{1,0,2:T(2,128)(2,1)S(1)} %get-tuple-element.20), channel_id=5, replica_groups=mesh['tm'=128,'head'=4] {'tm'}, dimensions={2}, use_global_device_ids=true | all-gather | bytes 990720 | tf_op jit(solution)/shard_map/all_gather | solution.py:71
  1410.6 2.5 copy.126
  1413.1 455.3 %all-gather.9.cloned.1.call-done = bf16[1,1920,3,256]{3,2,0,1:T(4,128)(2,1)} async-done(((bf16[1,15,3,256]{3,2,0,1:T(4,128)(2,1)}), bf16[1,1920,3,256]{3,2,0,1:T(4,128)(2,1)}) %all-gather.9.cloned.1.call-update) | async-done | bytes 2949136 | tf_op jit(solution)/shard_map/all_gather | solution.py:70
  1868.5 7.1 copy.123
  1875.6 145.2 %reduce-scatter.3.cloned.1.call-done = bf16[32,2,1920]{2,0,1:T(8,128)(2,1)} async-done(((bf16[128,2,1920]{2,0,1:T(8,128)(2,1)}), bf16[32,2,1920]{2,0,1:T(8,128)(2,1)}) %reduce-scatter.3.cloned.1.call-update) | async-done | bytes 245776 | tf_op jit(solution)/shard_map/reduce_scatter | solution.py:84
  2020.8 1.1 multiply_reduce_fusion
  2021.9 1.1 multiply_convert_fusion
  2023.0 31.7 %all_gather.21 = bf16[128,2,1920]{2,0,1:T(8,128)(2,1)S(1)} all-gather(bf16[32,2,1920]{2,0,1:T(8,128)(2,1)S(1)} %multiply_convert_fusion), channel_id=1, replica_groups=mesh['tm'=128,'head'=4] {'head'}, dimensions={0}, use_global_device_ids=true | all-gather | bytes 1228800 | tf_op jit(solution)/shard_map/all_gather | solution.py:66
  2054.6 1.0 copy.121
  2056.0 2.8 fusion.13
  2058.9 1.3 collective-permute-start.3
  2060.2 1.3 collective-permute-start.2
  2061.9 1.3 collective-permute-done.3
  2063.8 2.1 collective-permute-done.2
  2066.9 1.4 convolution_convert_fusion
  2068.3 72.4 %reduce-scatter.5.cloned.1.call-done = bf16[32,2,1920]{2,0,1:T(8,128)(2,1)} async-done(((bf16[128,2,1920]{2,0,1:T(8,128)(2,1)}), bf16[32,2,1920]{2,0,1:T(8,128)(2,1)}) %reduce-scatter.5.cloned.1.call-update) | async-done | bytes 245776 | tf_op jit(solution)/shard_map/reduce_scatter | solution.py:84
  2140.7 1.0 add_convert_fusion
  (57 shorter events, 12.2 us)
Async XLA Ops:
  6.5 895.9 %all-gather.7.cloned.1.call-start = ((), (), s32[]{:S(2)}) async-start(), calls=%async_computation.6 | async-start | bytes 3962880 | tf_op jit(solution)/shard_map/all_gather | solution.py:70
  8.1 1860.3 %all-gather.9.cloned.1.call-start = ((), (), s32[]{:S(2)}) async-start(), calls=%async_computation.7 | async-start | bytes 3962880 | tf_op jit(solution)/shard_map/all_gather | solution.py:70
  10.8 55.7 %copy-start.1 = (bf16[2,256,15]{1,0,2:T(2,128)(2,1)S(1)}, bf16[2,256,15]{1,0,2:T(2,128)(2,1)}, u32[]{:S(2)}) copy-start(bf16[2,256,15]{1,0,2:T(2,128)(2,1)} %param.9) | copy-start | bytes 46084
  58.1 498.9 %all-to-all-start.1 = ((bf16[128,2,480]{2,1,0:T(2,128)(2,1)}), bf16[128,2,480]{2,1,0:T(2,128)(2,1)S(1)}, u32[]{:S(2)}, u32[]{:S(2)}) async-start(bf16[128,2,480]{2,1,0:T(2,128)(2,1)} %all_to_all.7), calls=%async_computation.1 | async-start | bytes 524288 | tf_op jit(solution)/shard_map/all_to_all | solution.py:52
  66.5 1954.3 %reduce-scatter.3.cloned.1.call-start = ((), (), s32[]{:S(2)}) async-start(), calls=%async_computation.4 | async-start | bytes 1228800 | tf_op jit(solution)/shard_map/reduce_scatter | solution.py:84
  67.2 489.8 %copy-start.2 = (f32[2,1920]{1,0:T(2,128)S(1)}, f32[2,1920]{1,0:T(2,128)}, u32[]{:S(2)}) copy-start(f32[2,1920]{1,0:T(2,128)} %param.7) | copy-start | bytes 46084
  912.5 3.2 collective-permute-start.1
  913.8 3.3 collective-permute-start
  919.4 1221.3 %reduce-scatter.5.cloned.1.call-start = ((), (), s32[]{:S(2)}) async-start(), calls=%async_computation.5 | async-start | bytes 1228800 | tf_op jit(solution)/shard_map/reduce_scatter | solution.py:84
  2058.9 4.3 collective-permute-start.3
  2060.2 5.8 collective-permute-start.2
  2066.5 74.2 %copy-start = (bf16[32,2,1920]{2,0,1:T(8,128)(2,1)S(1)}, bf16[32,2,1920]{2,0,1:T(8,128)(2,1)}, u32[]{:S(2)}) copy-start(bf16[32,2,1920]{2,0,1:T(8,128)(2,1)} %reduce-scatter.3.cloned.1.call-done) | copy-start | bytes 737284
Sparse Core Ops, SparseCore 0:
  9.4 892.9 all-gather.6
  904.5 963.9 all-gather.8
  1871.6 149.1 reduce-scatter.2
  2068.4 72.1 reduce-scatter.4
where the time goes:
time: 2150 us
  blocking collectives  1130 us (53%)
  waiting for transfers between devices  946 us (44%)
  local copies, waits for them, and re-layouts  32 us (1%)
    all_gather x2, blocking collectives, local(): lax.all_gather(out_weight[layer_num], 'tm', axis=1, tiled=True)  978 us
    all_gather x2, waiting for transfers between devices, local(): lax.all_gather(qkv_weight[layer_num], 'tm', axis=0, tiled=True)  724 us
    reduce_scatter x2, waiting for transfers between devices, local(): lax.psum_scatter(partial_out.reshape(gathered.shape).astype(jnp.bfloat16)...  218 us
    all_gather x2, blocking collectives, local(): gathered = lax.all_gather(normed, 'head', axis=0, tiled=True)  106 us
  transfers between devices with their start and end apart: 9, of which 8 were waited for; matrix products, arithmetic and copies ran while one was open for 2% of the time, Pallas kernels for 0%

commit v1 on v0

v1 whole, which is shorter than its diff:
```python
import jax
import jax.numpy as jnp
from jax import lax
from jax.experimental import pallas as pl
from jax.experimental.pallas import tpu as pltpu
from jax.sharding import PartitionSpec as P

NX, NY, NZ, ZLO = 4, 4, 16, 8
LAYERS = 2
D = 1920
DP = 2048
QP = 512
EPSILON = 1e-06
F32, BF16 = jnp.float32, jnp.bfloat16
MESH = pl.DeviceIdType.MESH


def dot(a, b):
    return jnp.dot(a, b, preferred_element_type=F32)


def dot_t(a, b):
    return lax.dot_general(a, b, (((1,), (1,)), ((), ())), preferred_element_type=F32)


def iota(shape, dim):
    return lax.broadcasted_iota(jnp.int32, shape, dim)


def onehot(mask):
    return jnp.where(mask, 1.0, 0.0).astype(BF16)


def kernel(
    lat_ref, pad_ref, gain_ref, wloc_ref, out_ref,
    latp, r1, y1, xq, wz, wf, wos, resid, xn, qkv, pkv, blb, bls, gs, rsb, fo,
    az_s, az_r, ay_s, ay_r, wz_s, wz_r, wx_s, wx_r, wy_s, wy_r, wg_s, wg_r,
    wo_s, wo_r, ag_s, ag_r, kv_s, kv_r, bl_s, bl_r, rs_s, rs_r, fi_s, fi_r,
):
    tm, hd = lax.axis_index("tm"), lax.axis_index("head")
    y, x, zl = tm // 32, (tm // 8) % 4, tm % 8
    zh, c = hd // 2, hd % 2
    z = zh * 8 + zl

    def dev(xx, yy, zz, cc):
        return (yy * 32 + xx * 8 + zz % 8, (zz // 8) * 2 + cc)

    sends = []

    def send(src, dst, s_sem, r_sem, to):
        copy = pltpu.make_async_remote_copy(
            src_ref=src, dst_ref=dst, send_sem=s_sem, recv_sem=r_sem,
            device_id=to, device_id_type=MESH,
        )
        copy.start()
        sends.append(copy)

    def arrive(dst, sem):
        pltpu.make_async_copy(dst, dst, sem).wait()

    clip_x = z // 4
    pair = z % 4
    xu, xd, xo = (x + 1) % 4, (x + 3) % 4, (x + 2) % 4
    yu, yd, yo = (y + 1) % 4, (y + 3) % 4, (y + 2) % 4
    zu, zd = (z + 1) % 16, (z + 15) % 16

    barrier = pltpu.get_barrier_semaphore()

    def greet(to):
        pl.semaphore_signal(barrier, inc=1, device_id=to, device_id_type=MESH)

    for o in range(1, 16):
        greet(dev(x, y, (z + o) % 16, c))
    for o in range(4):
        for j in range(2):
            if o or j:
                greet(dev((x + o) % 4, y, z, (c + j) % 2))
    for o in range(1, 4):
        for j in range(2):
            greet(dev(x, (y + o) % 4, z, (c + j) % 2))
    for o in range(4):
        greet(dev((x + o) % 4, y, x * 4 + zl // 2, zl % 2))

    row, col = iota((256, 256), 0), iota((256, 256), 1)
    rows_by_z = onehot(col == ((row >> 2) & 3) * 64 + (row >> 4) * 4 + (row & 3))
    chan, pch = iota((480, QP), 0), iota((480, QP), 1)
    spread = onehot((chan == (pch >> 4) * 15 + (pch & 15)) & ((pch & 15) != 15))
    moved = dot(rows_by_z, lat_ref[...]).astype(BF16)
    moved = dot(moved, spread) + pad_ref[...]
    latp[...] = moved.astype(BF16).reshape(16, 16, QP)
    wz[0, z] = wloc_ref[0]
    wz[1, z] = wloc_ref[1]
    pl.semaphore_wait(barrier, 15 + 7 + 6 + 4)

    def chain_send(l, d, i):
        if d == 0:
            block, to = (z + 17 - i) % 16, dev(x, y, zu, c)
        else:
            block, to = (z + i - 1) % 16, dev(x, y, zd, c)
        send(wz.at[l, block], wz.at[l, block], wz_s.at[l, d, i - 1], wz_r.at[l, d, i - 1], to)

    def chain_step(l, i):
        arrive(wz.at[l, (z + 16 - i) % 16], wz_r.at[l, 0, i - 1])
        if i < 8:
            chain_send(l, 0, i + 1)
            arrive(wz.at[l, (z + i) % 16], wz_r.at[l, 1, i - 1])
            if i < 7:
                chain_send(l, 1, i + 1)

    def scatter_send(l):
        for a in range(2):
            half = (x // 2 + a) % 2
            t = half * 2 + c
            for b in range(2):
                j = (c + b) % 2
                src = wz.at[l, pl.ds(half * 8, 8), j]
                dst = wf.at[l, y, x]
                copy = pltpu.make_async_remote_copy(
                    src_ref=src, dst_ref=dst, send_sem=wx_s.at[l, a * 2 + b], recv_sem=wx_r.at[l, x],
                    device_id=dev(t, y, z, j), device_id_type=MESH,
                )
                if a == 0 and b == 0:
                    own = pltpu.make_async_copy(src, dst, wx_r.at[l, x])

                    @pl.when(c == x % 2)
                    def _():
                        own.start()

                    @pl.when(c != x % 2)
                    def _():
                        copy.start()

                    scattered.append(copy)
                else:
                    copy.start()
                    sends.append(copy)

    scattered = []

    def piece(l, yy, xx):
        return wf.at[l, yy, xx]

    def ring_send(l):
        for p in range(4):
            arrive(piece(l, y, p), wx_r.at[l, p])
            for d, to in ((0, yu), (1, yd)):
                send(piece(l, y, p), piece(l, y, p), wy_s.at[l, d, p], wy_r.at[l, d, p], dev(x, to, z, c))

    def ring_forward(l):
        for p in range(4):
            arrive(piece(l, yd, p), wy_r.at[l, 0, p])
            if p < 2:
                send(piece(l, yd, p), piece(l, yd, p), wg_s.at[l, p], wg_r.at[l, p], dev(x, yu, z, c))
            arrive(piece(l, yu, p), wy_r.at[l, 1, p])
            if p >= 2:
                send(piece(l, yu, p), piece(l, yu, p), wg_s.at[l, p], wg_r.at[l, p], dev(x, yd, z, c))

    def ring_end(l):
        for p in range(4):
            arrive(piece(l, yo, p), wg_r.at[l, p])
        send(wf.at[l, :, :, :, :, pl.ds(384, 128)], wos.at[l], wo_s.at[l], wo_r.at[l], dev(x, y, z, 1 - c))

    chain_send(0, 0, 1)
    chain_send(0, 1, 1)
    own_z = pltpu.make_async_copy(latp.at[z], r1.at[z], az_r.at[0])
    own_z.start()
    for o in range(1, 16):
        to = (z + o) % 16
        send(latp.at[to], r1.at[z], az_s.at[o], az_r.at[o], dev(x, y, to, c))

    for i in range(1, 9):
        chain_step(0, i)
    scatter_send(0)

    own_z.wait()
    for o in range(1, 16):
        arrive(r1.at[(z + 16 - o) % 16], az_r.at[o])
    rows_by_y = onehot(col == ((row >> 1) & 15) * 16 + (row >> 5) * 2 + (row & 1))
    y1[...] = dot(rows_by_y, r1[...].reshape(256, QP)).astype(BF16).reshape(8, 2, 16, QP)
    own_y = pltpu.make_async_copy(y1.at[y * 2 + c], xq.at[:, c, y], ay_r.at[0])
    own_y.start()
    for o in range(4):
        for j in range(2):
            if o or j:
                to, par = (y + o) % 4, (c + j) % 2
                send(
                    y1.at[to * 2 + par], xq.at[:, c, y], ay_s.at[o * 2 + j], ay_r.at[o * 2 + j],
                    dev(x, to, z, par),
                )
    chain_send(1, 0, 1)
    chain_send(1, 1, 1)
    ring_send(0)

    own_y.wait()
    for o in range(4):
        for j in range(2):
            if o or j:
                arrive(xq.at[:, (c + j) % 2, (y + 4 - o) % 4], ay_r.at[o * 2 + j])
    for h in range(4):
        resid[:, h * QP:(h + 1) * QP] = xq[h // 2, h % 2].reshape(64, QP).astype(F32)

    real = (iota((1, DP), 1) & 15) != 15

    def norm_rows(l):
        rows = resid[...]
        square = jnp.where(real, rows * rows, 0.0)
        mean_square = jnp.sum(square, axis=1, keepdims=True) * (1.0 / D)
        normed = jnp.where(real, rows * lax.rsqrt(mean_square + EPSILON) * gain_ref[l], rows)
        xn[l, c, x] = normed.astype(BF16).reshape(4, 16, DP)

    def gather_send(l):
        mine = xn.at[l, c, x]
        send(mine, mine, ag_s.at[l, 0], ag_r.at[l, 0], dev(xu, y, z, c))
        send(mine, mine, ag_s.at[l, 1], ag_r.at[l, 1], dev(xd, y, z, c))
        send(mine, mine, ag_s.at[l, 2], ag_r.at[l, 2], dev(x, y, z, 1 - c))

    def gather_forward(l):
        sibling = dev(x, y, z, 1 - c)
        low, high = pl.ds(0, 2), pl.ds(2, 2)
        block = xn.at[l, c, xd]
        arrive(block, ag_r.at[l, 0])
        send(xn.at[l, c, xd, low], xn.at[l, c, xd, low], ag_s.at[l, 3], ag_r.at[l, 3], dev(xu, y, z, c))
        send(block, block, ag_s.at[l, 4], ag_r.at[l, 4], sibling)
        block = xn.at[l, c, xu]
        arrive(block, ag_r.at[l, 1])
        send(xn.at[l, c, xu, high], xn.at[l, c, xu, high], ag_s.at[l, 5], ag_r.at[l, 5], dev(xd, y, z, c))
        send(block, block, ag_s.at[l, 6], ag_r.at[l, 6], sibling)

    def gather_end(l):
        sibling = dev(x, y, z, 1 - c)
        low, high = pl.ds(0, 2), pl.ds(2, 2)
        for part, got, to in ((low, 3, 7), (high, 5, 8)):
            block = xn.at[l, c, xo, part]
            arrive(block, ag_r.at[l, got])
            send(block, block, ag_s.at[l, to], ag_r.at[l, to], sibling)
        arrive(xn.at[l, 1 - c, x], ag_r.at[l, 2])
        arrive(xn.at[l, 1 - c, xd], ag_r.at[l, 4])
        arrive(xn.at[l, 1 - c, xu], ag_r.at[l, 6])
        arrive(xn.at[l, 1 - c, xo, low], ag_r.at[l, 7])
        arrive(xn.at[l, 1 - c, xo, high], ag_r.at[l, 8])

    def project(l):
        weight = wf[l].reshape(DP, QP)[:, :384]
        for p in range(2):
            qkv[p] = dot(xn[l, p].reshape(256, DP), weight).astype(BF16)

    lane = iota((1, 128), 1)
    frame = iota((1, 256), 1) & 1

    def first_frame(p):
        tile = xn[0, p, clip_x, y, :, :128].astype(F32)
        spot = (iota((16, 128), 0) == (pair * 2 + p) * 2) & (iota((16, 128), 1) == 15)
        kept = jnp.where(spot, tile, 0.0)
        return jnp.sum(jnp.sum(kept, axis=1, keepdims=True), axis=0, keepdims=True)

    def attend(p, prev_keys, prev_values, visible):
        queries = qkv[p, :, :128] * jnp.asarray(0.125, BF16)
        keys, values = qkv[p, :, 128:256], qkv[p, :, 256:384]
        parts = []
        for hh in range(2):
            mine = (lane // 64) == hh
            q = jnp.where(mine, queries, jnp.zeros_like(queries))
            own = dot_t(q, keys)
            past = jnp.where(visible, dot_t(q, prev_keys), -jnp.inf)
            highest = jnp.maximum(jnp.max(own, axis=1, keepdims=True), jnp.max(past, axis=1, keepdims=True))
            own, past = jnp.exp(own - highest), jnp.exp(past - highest)
            scale = 1.0 / (jnp.sum(own, axis=1, keepdims=True) + jnp.sum(past, axis=1, keepdims=True))
            parts.append(
                dot((own * scale).astype(BF16), values) + dot((past * scale).astype(BF16), prev_values)
            )
        return jnp.where(lane < 64, parts[0], parts[1]).astype(BF16)

    gather_like = pl.ds(128, 256)
    norm_rows(0)
    gather_send(0)
    ring_forward(0)
    gather_forward(0)
    gather_end(0)
    ring_end(0)
    starts = [first_frame(p) for p in range(2)]

    for l in range(LAYERS):
        project(l)
        send(qkv.at[1, :, gather_like], pkv.at[l], kv_s.at[l], kv_r.at[l], dev(x, y, zu, c))
        see = frame.astype(F32) >= starts[1]
        blb[1] = attend(1, qkv[0, :, 128:256], qkv[0, :, 256:384], see)
        if l == 0:
            for i in range(1, 9):
                chain_step(1, i)
            scatter_send(1)
        arrive(pkv.at[l], kv_r.at[l])
        see = (frame.astype(F32) >= starts[0]) & (pair > 0)
        blb[0] = attend(0, pkv[l, :, :128], pkv[l, :, 128:], see)
        send(blb.at[1 - c], bls.at[l], bl_s.at[l], bl_r.at[l], dev(x, y, z, 1 - c))
        if l == 0:
            ring_send(1)
        arrive(bls.at[l], bl_r.at[l])
        arrive(wos.at[l], wo_r.at[l])
        blended = jnp.concatenate([blb[c], bls[l]], axis=1)
        weight = jnp.concatenate([wf[l, :, :, :, :, 384:], wos[l]], axis=4).reshape(DP, 256)
        gs[l] = dot_t(blended, weight).astype(BF16).reshape(4, 64, DP)
        for o in range(1, 4):
            to = (x + o) % 4
            send(gs.at[l, to], rsb.at[l, o - 1], rs_s.at[l, o - 1], rs_r.at[l, o - 1], dev(to, y, z, c))
        if l == 0:
            ring_forward(1)
        for o in range(1, 4):
            arrive(rsb.at[l, o - 1], rs_r.at[l, o - 1])
        total = gs[l, x].astype(F32) + rsb[l, 0].astype(F32) + rsb[l, 1].astype(F32) + rsb[l, 2].astype(F32)
        resid[...] += total
        if l == 0:
            norm_rows(1)
            gather_send(1)
            drain_upto = len(sends)
            gather_forward(1)
            gather_end(1)
            ring_end(1)
            for copy in sends[:drain_upto]:
                copy.wait_send()
            del sends[:drain_upto]

    refined = resid[...].astype(BF16)
    for b in range(D // 128):
        first = ((b * 128 // 15) * 16 + (b * 128) % 15) // 128 * 128
        width = min(384, DP - first)
        a, ch = iota((width, 128), 0) + first, iota((width, 128), 1) + b * 128
        group = (ch * 4370) >> 16
        pick = onehot(a == group * 16 + (ch - group * 15))
        fo[:, :, b * 128:(b + 1) * 128] = dot(refined[:, first:first + width], pick).astype(BF16).reshape(4, 16, 128)
    last = []
    stretch = pair * 2 + c
    for q in range(4):
        to_z = stretch + 8 * (q // 2)
        copy = pltpu.make_async_remote_copy(
            src_ref=fo.at[q], dst_ref=out_ref.at[x], send_sem=fi_s.at[q], recv_sem=fi_r.at[x],
            device_id=dev(clip_x, y, to_z, q % 2), device_id_type=MESH,
        )
        own = pltpu.make_async_copy(fo.at[q], out_ref.at[x], fi_r.at[x])
        here = (clip_x == x) & (to_z == z) & (c == q % 2)
        last.append((copy, here))

        @pl.when(here)
        def _():
            own.start()

        @pl.when(jnp.logical_not(here))
        def _():
            copy.start()

    for p in range(4):
        arrive(out_ref.at[p], fi_r.at[p])
    for copy, here in last:

        @pl.when(jnp.logical_not(here))
        def _():
            copy.wait_send()

    for copy in scattered:

        @pl.when(c != x % 2)
        def _():
            copy.wait_send()

    for copy in sends:
        copy.wait_send()


def local(latent, start_frame, norm_gains, qkv_weight, out_weight):
    pad_row = jnp.where(jnp.arange(QP) % 16 == 15, start_frame[0].astype(F32), 0.0)[None, :]
    gains = jnp.pad(norm_gains.reshape(LAYERS, 128, 15), ((0, 0), (0, 0), (0, 1))).reshape(LAYERS, 1, DP)
    both = jnp.concatenate([qkv_weight, out_weight.transpose(0, 2, 1)[:, :, None, :]], axis=2)
    both = both.reshape(LAYERS, 15, 4, 2, 128).transpose(0, 3, 1, 2, 4).reshape(LAYERS, 2, 15, QP)
    both = jnp.pad(both, ((0, 0), (0, 0), (0, 1), (0, 0)))
    dma = pltpu.SemaphoreType.DMA
    vmem = pltpu.VMEM
    out = pl.pallas_call(
        kernel,
        out_shape=jax.ShapeDtypeStruct((4, 16, D), BF16),
        in_specs=[pl.BlockSpec(memory_space=vmem)] * 4,
        out_specs=pl.BlockSpec(memory_space=vmem),
        scratch_shapes=[
            vmem((16, 16, QP), BF16),
            vmem((16, 16, QP), BF16),
            vmem((8, 2, 16, QP), BF16),
            vmem((2, 2, 4, 16, QP), BF16),
            vmem((LAYERS, 16, 2, 16, QP), BF16),
            vmem((LAYERS, 4, 4, 8, 16, QP), BF16),
            vmem((LAYERS, 4, 4, 8, 16, 128), BF16),
            vmem((64, DP), F32),
            vmem((LAYERS, 2, 4, 4, 16, DP), BF16),
            vmem((2, 256, 384), BF16),
            vmem((LAYERS, 256, 256), BF16),
            vmem((2, 256, 128), BF16),
            vmem((LAYERS, 256, 128), BF16),
            vmem((LAYERS, 4, 64, DP), BF16),
            vmem((LAYERS, 3, 64, DP), BF16),
            vmem((4, 16, D), BF16),
            dma((16,)), dma((16,)), dma((8,)), dma((8,)),
            dma((LAYERS, 2, 8)), dma((LAYERS, 2, 8)), dma((LAYERS, 4)), dma((LAYERS, 4)),
            dma((LAYERS, 2, 4)), dma((LAYERS, 2, 4)), dma((LAYERS, 4)), dma((LAYERS, 4)),
            dma((LAYERS,)), dma((LAYERS,)), dma((LAYERS, 9)), dma((LAYERS, 9)),
            dma((LAYERS,)), dma((LAYERS,)), dma((LAYERS,)), dma((LAYERS,)),
            dma((LAYERS, 3)), dma((LAYERS, 3)), dma((4,)), dma((4,)),
        ],
        compiler_params=pltpu.CompilerParams(
            collective_id=0, has_side_effects=True, vmem_limit_bytes=56 * 2**20
        ),
    )(latent[0], pad_row, gains, both)
    return out.reshape(32, 2, D)


def solution(mesh):
    return jax.shard_map(
        local,
        mesh=mesh,
        in_specs=(
            P("tm", None, "head"),
            P("tm"),
            P(),
            P(None, "tm", None, "head"),
            P(None, "head", "tm"),
        ),
        out_specs=P("head", "tm", None),
        check_vma=False,
    )
```

time: 2150 us -> 180 us (0.08)
  the two profiles are of different devices: /device:TPU:1 before, /device:TPU:3 now
where the time goes in v1:
time: 180 us
  Pallas kernels  174 us (97%)
  local copies, waits for them, and re-layouts  5.16 us (3%)
    pallas_call x1, Pallas kernels, local(): pl.pallas_call(kernel, out_shape=jax.ShapeDtypeStruct((4, 16, D), BF16),...  174 us

profile of v1, /device:TPU:3, one launch (start us, length us, event | category | flops | bytes accessed | tf_op | source)
XLA Modules:
  0.0 180.1 jit_solution(3662974431961394347)
XLA Ops:
  0.0 0.0 copy-start.1
  0.7 0.6 compare_select_fusion.pad_ref
  1.2 0.8 concatenate.9
  2.0 0.0 copy-done.1
  2.0 0.1 concatenate.8
  2.2 0.1 maximum_bitcast_fusion
  2.3 0.0 copy-start.2
  2.3 0.6 pad.9.wloc_ref
  3.0 0.1 copy-done.2
  3.0 0.0 copy-start
  3.0 0.2 reshape.45
  3.3 0.7 reshape.49.gain_ref
  4.0 0.0 copy-done
  4.0 0.8 copy.9
  4.8 173.6 %shard_map.55 = bf16[4,16,1920]{2,1,0:T(8,128)(2,1)} custom-call(bf16[256,480]{1,0:T(8,128)(2,1)} %bitcast.11, f32[1,512]{1,0:T(1,128)} %compare_select_fusion.pad_ref, f32[2,1,2048]{2,1,0:T(1,128)} %reshape.49.gain_ref, bf16[2,2,16,512]{3,2,1,0:T(8,128)(2,1)} %pad.9.wloc_ref), custom_call_target="tpu_custom_call" | custom-call | tf_op jit(solution)/shard_map/pallas_call | solution.py:376
  178.4 1.7 reshape.48
  (5 shorter events, 0.1 us)
Async XLA Ops:
  0.0 2.0 %copy-start.1 = (bf16[2,15,3,256]{3,0,2,1:T(2,128)(2,1)S(1)}, bf16[2,15,3,256]{3,0,2,1:T(2,128)(2,1)}, u32[]{:S(2)}) copy-start(bf16[2,15,3,256]{3,0,2,1:T(2,128)(2,1)} %param.8) | copy-start | bytes 138244
  2.3 0.7 copy-start.2
  3.0 1.0 copy-start

commit v2 on v1

--- a/solution.py
+++ b/solution.py
@@ -33,7 +33,7 @@
 
 def kernel(
     lat_ref, pad_ref, gain_ref, wloc_ref, out_ref,
-    latp, r1, y1, xq, wz, wf, wos, resid, xn, qkv, pkv, blb, bls, gs, rsb, fo,
+    latp, r1, y1, xq, wz, wf, wos, resid, xn, qkv, pkv, blb, bls, gs, rsb, rst, rso, fo,
     az_s, az_r, ay_s, ay_r, wz_s, wz_r, wx_s, wx_r, wy_s, wy_r, wg_s, wg_r,
     wo_s, wo_r, ag_s, ag_r, kv_s, kv_r, bl_s, bl_r, rs_s, rs_r, fi_s, fi_r,
 ):
@@ -140,37 +140,49 @@
     def piece(l, yy, xx):
         return wf.at[l, yy, xx]
 
-    def ring_send(l):
+    def lanes(l, yy, xx, part):
+        return wf.at[l, yy, xx, :, :, pl.ds(0, 384) if part == 0 else pl.ds(384, 128)]
+
+    def ring_send(l, part):
         for p in range(4):
-            arrive(piece(l, y, p), wx_r.at[l, p])
+            if part == 0:
+                arrive(piece(l, y, p), wx_r.at[l, p])
+            block = lanes(l, y, p, part)
             for d, to in ((0, yu), (1, yd)):
-                send(piece(l, y, p), piece(l, y, p), wy_s.at[l, d, p], wy_r.at[l, d, p], dev(x, to, z, c))
-
-    def ring_forward(l):
+                send(block, block, wy_s.at[l, part, d, p], wy_r.at[l, part, d, p], dev(x, to, z, c))
+
+    def ring_forward(l, part, p):
+        below, above = lanes(l, yd, p, part), lanes(l, yu, p, part)
+        arrive(below, wy_r.at[l, part, 0, p])
+        if p < 2:
+            send(below, below, wg_s.at[l, part, p], wg_r.at[l, part, p], dev(x, yu, z, c))
+        arrive(above, wy_r.at[l, part, 1, p])
+        if p >= 2:
+            send(above, above, wg_s.at[l, part, p], wg_r.at[l, part, p], dev(x, yd, z, c))
+
+    def ring_end(l, part):
         for p in range(4):
-            arrive(piece(l, yd, p), wy_r.at[l, 0, p])
-            if p < 2:
-                send(piece(l, yd, p), piece(l, yd, p), wg_s.at[l, p], wg_r.at[l, p], dev(x, yu, z, c))
-            arrive(piece(l, yu, p), wy_r.at[l, 1, p])
-            if p >= 2:
-                send(piece(l, yu, p), piece(l, yu, p), wg_s.at[l, p], wg_r.at[l, p], dev(x, yd, z, c))
-
-    def ring_end(l):
-        for p in range(4):
-            arrive(piece(l, yo, p), wg_r.at[l, p])
-        send(wf.at[l, :, :, :, :, pl.ds(384, 128)], wos.at[l], wo_s.at[l], wo_r.at[l], dev(x, y, z, 1 - c))
+            arrive(lanes(l, yo, p, part), wg_r.at[l, part, p])
+        if part == 1:
+            send(wf.at[l, :, :, :, :, pl.ds(384, 128)], wos.at[l], wo_s.at[l], wo_r.at[l], dev(x, y, z, 1 - c))
 
     chain_send(0, 0, 1)
     chain_send(0, 1, 1)
     own_z = pltpu.make_async_copy(latp.at[z], r1.at[z], az_r.at[0])
     own_z.start()
-    for o in range(1, 16):
+
+    def latent_send(o):
         to = (z + o) % 16
         send(latp.at[to], r1.at[z], az_s.at[o], az_r.at[o], dev(x, y, to, c))
 
     for i in range(1, 9):
+        latent_send(9 - i)
+        if i > 1:
+            latent_send(7 + i)
         chain_step(0, i)
     scatter_send(0)
+    chain_send(1, 0, 1)
+    chain_send(1, 1, 1)
 
     own_z.wait()
     for o in range(1, 16):
@@ -187,9 +199,9 @@
                     y1.at[to * 2 + par], xq.at[:, c, y], ay_s.at[o * 2 + j], ay_r.at[o * 2 + j],
                     dev(x, to, z, par),
                 )
-    chain_send(1, 0, 1)
-    chain_send(1, 1, 1)
-    ring_send(0)
+    chain_step(1, 1)
+    ring_send(0, 0)
+    chain_step(1, 2)
 
     own_y.wait()
     for o in range(4):
@@ -208,41 +220,51 @@
         normed = jnp.where(real, rows * lax.rsqrt(mean_square + EPSILON) * gain_ref[l], rows)
         xn[l, c, x] = normed.astype(BF16).reshape(4, 16, DP)
 
+    low, high = pl.ds(0, 2), pl.ds(2, 2)
+
+    def gather_copy(l, block, n, to):
+        send(block, block, ag_s.at[l, n], ag_r.at[l, n], to)
+
     def gather_send(l):
-        mine = xn.at[l, c, x]
-        send(mine, mine, ag_s.at[l, 0], ag_r.at[l, 0], dev(xu, y, z, c))
-        send(mine, mine, ag_s.at[l, 1], ag_r.at[l, 1], dev(xd, y, z, c))
-        send(mine, mine, ag_s.at[l, 2], ag_r.at[l, 2], dev(x, y, z, 1 - c))
+        up, down = dev(xu, y, z, c), dev(xd, y, z, c)
+        gather_copy(l, xn.at[l, c, x, low], 0, up)
+        gather_copy(l, xn.at[l, c, x, high], 1, down)
+        gather_copy(l, xn.at[l, c, x, high], 2, up)
+        gather_copy(l, xn.at[l, c, x, low], 3, down)
+        gather_copy(l, xn.at[l, c, x], 4, dev(x, y, z, 1 - c))
 
     def gather_forward(l):
+        arrive(xn.at[l, c, xd, low], ag_r.at[l, 0])
+        gather_copy(l, xn.at[l, c, xd, low], 5, dev(xu, y, z, c))
+        arrive(xn.at[l, c, xu, high], ag_r.at[l, 1])
+        gather_copy(l, xn.at[l, c, xu, high], 6, dev(xd, y, z, c))
+
+    def gather_sides(l):
         sibling = dev(x, y, z, 1 - c)
-        low, high = pl.ds(0, 2), pl.ds(2, 2)
-        block = xn.at[l, c, xd]
-        arrive(block, ag_r.at[l, 0])
-        send(xn.at[l, c, xd, low], xn.at[l, c, xd, low], ag_s.at[l, 3], ag_r.at[l, 3], dev(xu, y, z, c))
-        send(block, block, ag_s.at[l, 4], ag_r.at[l, 4], sibling)
-        block = xn.at[l, c, xu]
-        arrive(block, ag_r.at[l, 1])
-        send(xn.at[l, c, xu, high], xn.at[l, c, xu, high], ag_s.at[l, 5], ag_r.at[l, 5], dev(xd, y, z, c))
-        send(block, block, ag_s.at[l, 6], ag_r.at[l, 6], sibling)
+        arrive(xn.at[l, c, xd, high], ag_r.at[l, 2])
+        gather_copy(l, xn.at[l, c, xd], 7, sibling)
+        arrive(xn.at[l, c, xu, low], ag_r.at[l, 3])
+        gather_copy(l, xn.at[l, c, xu], 8, sibling)
+
+    def gather_far(l):
+        sibling = dev(x, y, z, 1 - c)
+        arrive(xn.at[l, c, xo, low], ag_r.at[l, 5])
+        gather_copy(l, xn.at[l, c, xo, low], 9, sibling)
+        arrive(xn.at[l, c, xo, high], ag_r.at[l, 6])
+        gather_copy(l, xn.at[l, c, xo, high], 10, sibling)
 
     def gather_end(l):
-        sibling = dev(x, y, z, 1 - c)
-        low, high = pl.ds(0, 2), pl.ds(2, 2)
-        for part, got, to in ((low, 3, 7), (high, 5, 8)):
-            block = xn.at[l, c, xo, part]
-            arrive(block, ag_r.at[l, got])
-            send(block, block, ag_s.at[l, to], ag_r.at[l, to], sibling)
-        arrive(xn.at[l, 1 - c, x], ag_r.at[l, 2])
-        arrive(xn.at[l, 1 - c, xd], ag_r.at[l, 4])
-        arrive(xn.at[l, 1 - c, xu], ag_r.at[l, 6])
-        arrive(xn.at[l, 1 - c, xo, low], ag_r.at[l, 7])
-        arrive(xn.at[l, 1 - c, xo, high], ag_r.at[l, 8])
+        arrive(xn.at[l, 1 - c, x], ag_r.at[l, 4])
+        arrive(xn.at[l, 1 - c, xd], ag_r.at[l, 7])
+        arrive(xn.at[l, 1 - c, xu], ag_r.at[l, 8])
+        arrive(xn.at[l, 1 - c, xo, low], ag_r.at[l, 9])
+        arrive(xn.at[l, 1 - c, xo, high], ag_r.at[l, 10])
 
     def project(l):
-        weight = wf[l].reshape(DP, QP)[:, :384]
-        for p in range(2):
-            qkv[p] = dot(xn[l, p].reshape(256, DP), weight).astype(BF16)
+        weight = wf[l, :, :, :, :, :384].reshape(DP, 384)
+        qkv[c] = dot(xn[l, c].reshape(256, DP), weight).astype(BF16)
+        gather_end(l)
+        qkv[1 - c] = dot(xn[l, 1 - c].reshape(256, DP), weight).astype(BF16)
 
     lane = iota((1, 128), 1)
     frame = iota((1, 256), 1) & 1
@@ -273,51 +295,91 @@
     gather_like = pl.ds(128, 256)
     norm_rows(0)
     gather_send(0)
-    ring_forward(0)
+    chain_step(1, 3)
+    ring_forward(0, 0, 0)
     gather_forward(0)
-    gather_end(0)
-    ring_end(0)
-    starts = [first_frame(p) for p in range(2)]
+    chain_step(1, 4)
+    ring_forward(0, 0, 1)
+    gather_sides(0)
+    chain_step(1, 5)
+    ring_forward(0, 0, 2)
+    gather_far(0)
+    chain_step(1, 6)
+    ring_forward(0, 0, 3)
+    ring_send(0, 1)
+    chain_step(1, 7)
+    chain_step(1, 8)
+    scatter_send(1)
+    ring_end(0, 0)
 
     for l in range(LAYERS):
         project(l)
         send(qkv.at[1, :, gather_like], pkv.at[l], kv_s.at[l], kv_r.at[l], dev(x, y, zu, c))
+        if l == 0:
+            starts = [first_frame(p) for p in range(2)]
         see = frame.astype(F32) >= starts[1]
-        blb[1] = attend(1, qkv[0, :, 128:256], qkv[0, :, 256:384], see)
+        blb[1] = attend(1, qkv[0, :, 128:256], qkv[0, :, 256:384], see).reshape(4, 64, 128)
         if l == 0:
-            for i in range(1, 9):
-                chain_step(1, i)
-            scatter_send(1)
+            for p in range(4):
+                ring_forward(0, 1, p)
+            ring_send(1, 0)
         arrive(pkv.at[l], kv_r.at[l])
         see = (frame.astype(F32) >= starts[0]) & (pair > 0)
-        blb[0] = attend(0, pkv[l, :, :128], pkv[l, :, 128:], see)
+        blb[0] = attend(0, pkv[l, :, :128], pkv[l, :, 128:], see).reshape(4, 64, 128)
         send(blb.at[1 - c], bls.at[l], bl_s.at[l], bl_r.at[l], dev(x, y, z, 1 - c))
         if l == 0:
-            ring_send(1)
+            ring_end(0, 1)
         arrive(bls.at[l], bl_r.at[l])
         arrive(wos.at[l], wo_r.at[l])
-        blended = jnp.concatenate([blb[c], bls[l]], axis=1)
         weight = jnp.concatenate([wf[l, :, :, :, :, 384:], wos[l]], axis=4).reshape(DP, 256)
-        gs[l] = dot_t(blended, weight).astype(BF16).reshape(4, 64, DP)
-        for o in range(1, 4):
-            to = (x + o) % 4
-            send(gs.at[l, to], rsb.at[l, o - 1], rs_s.at[l, o - 1], rs_r.at[l, o - 1], dev(to, y, z, c))
+
+        def update(to):
+            blended = jnp.concatenate([blb[c, to], bls[l, to]], axis=1)
+            gs[l, to] = dot_t(blended, weight).astype(BF16)
+
+        up, down = dev(xu, y, z, c), dev(xd, y, z, c)
+        first, second = pl.ds(0, 32), pl.ds(32, 32)
+
+        def scatter_copy(src, dst, n, to):
+            send(src, dst, rs_s.at[l, n], rs_r.at[l, n], to)
+
+        update(xo)
+        scatter_copy(gs.at[l, xo, first], rst.at[l, 0], 0, up)
+        scatter_copy(gs.at[l, xo, second], rst.at[l, 1], 1, down)
+        update(xu)
+        scatter_copy(gs.at[l, xu, second], rsb.at[l, 0, second], 2, up)
+        update(xd)
+        scatter_copy(gs.at[l, xd, first], rsb.at[l, 1, first], 3, down)
+        arrive(rst.at[l, 0], rs_r.at[l, 0])
+        rso[l, 0] = (gs[l, xu, :32].astype(F32) + rst[l, 0].astype(F32)).astype(BF16)
+        scatter_copy(rso.at[l, 0], rsb.at[l, 0, first], 4, up)
+        arrive(rst.at[l, 1], rs_r.at[l, 1])
+        rso[l, 1] = (gs[l, xd, 32:].astype(F32) + rst[l, 1].astype(F32)).astype(BF16)
+        scatter_copy(rso.at[l, 1], rsb.at[l, 1, second], 5, down)
+        update(x)
         if l == 0:
-            ring_forward(1)
-        for o in range(1, 4):
-            arrive(rsb.at[l, o - 1], rs_r.at[l, o - 1])
-        total = gs[l, x].astype(F32) + rsb[l, 0].astype(F32) + rsb[l, 1].astype(F32) + rsb[l, 2].astype(F32)
-        resid[...] += total
+            for p in range(4):
+                ring_forward(1, 0, p)
+            ring_send(1, 1)
+        arrive(rsb.at[l, 0, second], rs_r.at[l, 2])
+        arrive(rsb.at[l, 1, first], rs_r.at[l, 3])
+        arrive(rsb.at[l, 0, first], rs_r.at[l, 4])
+        arrive(rsb.at[l, 1, second], rs_r.at[l, 5])
+        resid[...] += gs[l, x].astype(F32) + rsb[l, 0].astype(F32) + rsb[l, 1].astype(F32)
         if l == 0:
             norm_rows(1)
             gather_send(1)
             drain_upto = len(sends)
             gather_forward(1)
-            gather_end(1)
-            ring_end(1)
+            gather_sides(1)
             for copy in sends[:drain_upto]:
                 copy.wait_send()
             del sends[:drain_upto]
+            gather_far(1)
+            for p in range(4):
+                ring_forward(1, 1, p)
+            ring_end(1, 0)
+            ring_end(1, 1)
 
     refined = resid[...].astype(BF16)
     for b in range(D // 128):
@@ -390,17 +452,19 @@
             vmem((LAYERS, 2, 4, 4, 16, DP), BF16),
             vmem((2, 256, 384), BF16),
             vmem((LAYERS, 256, 256), BF16),
-            vmem((2, 256, 128), BF16),
-            vmem((LAYERS, 256, 128), BF16),
+            vmem((2, 4, 64, 128), BF16),
+            vmem((LAYERS, 4, 64, 128), BF16),
             vmem((LAYERS, 4, 64, DP), BF16),
-            vmem((LAYERS, 3, 64, DP), BF16),
+            vmem((LAYERS, 2, 64, DP), BF16),
+            vmem((LAYERS, 2, 32, DP), BF16),
+            vmem((LAYERS, 2, 32, DP), BF16),
             vmem((4, 16, D), BF16),
             dma((16,)), dma((16,)), dma((8,)), dma((8,)),
             dma((LAYERS, 2, 8)), dma((LAYERS, 2, 8)), dma((LAYERS, 4)), dma((LAYERS, 4)),
-            dma((LAYERS, 2, 4)), dma((LAYERS, 2, 4)), dma((LAYERS, 4)), dma((LAYERS, 4)),
-            dma((LAYERS,)), dma((LAYERS,)), dma((LAYERS, 9)), dma((LAYERS, 9)),
+            dma((LAYERS, 2, 2, 4)), dma((LAYERS, 2, 2, 4)), dma((LAYERS, 2, 4)), dma((LAYERS, 2, 4)),
+            dma((LAYERS,)), dma((LAYERS,)), dma((LAYERS, 11)), dma((LAYERS, 11)),
             dma((LAYERS,)), dma((LAYERS,)), dma((LAYERS,)), dma((LAYERS,)),
-            dma((LAYERS, 3)), dma((LAYERS, 3)), dma((4,)), dma((4,)),
+            dma((LAYERS, 6)), dma((LAYERS, 6)), dma((4,)), dma((4,)),
         ],
         compiler_params=pltpu.CompilerParams(
             collective_id=0, has_side_effects=True, vmem_limit_bytes=56 * 2**20

time: 180 us -> 151 us (0.84)
  the two profiles are of different devices: /device:TPU:3 before, /device:TPU:13 now
where the time goes in v2:
time: 151 us
  Pallas kernels  144 us (95%)
  local copies, waits for them, and re-layouts  5.16 us (3%)
    pallas_call x1, Pallas kernels, local(): pl.pallas_call(kernel, out_shape=jax.ShapeDtypeStruct((4, 16, D), BF16),...  144 us

profile of v2, /device:TPU:13, one launch (start us, length us, event | category | flops | bytes accessed | tf_op | source)
XLA Modules:
  0.0 151.0 jit_solution(12503734152139530837)
XLA Ops:
  0.0 0.0 copy-start.1
  0.7 0.6 compare_select_fusion.pad_ref
  1.2 0.8 concatenate.9
  2.0 0.0 copy-done.1
  2.0 0.1 concatenate.8
  2.2 0.1 maximum_bitcast_fusion
  2.3 0.0 copy-start.2
  2.3 0.6 pad.9.wloc_ref
  3.0 0.1 copy-done.2
  3.0 0.0 copy-start
  3.0 0.2 reshape.45
  3.3 0.7 reshape.49.gain_ref
  4.0 0.0 copy-done
  4.0 0.8 copy.9
  4.8 144.4 %shard_map.55 = bf16[4,16,1920]{2,1,0:T(8,128)(2,1)} custom-call(bf16[256,480]{1,0:T(8,128)(2,1)} %bitcast.11, f32[1,512]{1,0:T(1,128)} %compare_select_fusion.pad_ref, f32[2,1,2048]{2,1,0:T(1,128)} %reshape.49.gain_ref, bf16[2,2,16,512]{3,2,1,0:T(8,128)(2,1)} %pad.9.wloc_ref), custom_call_target="tpu_custom_call" | custom-call | tf_op jit(solution)/shard_map/pallas_call | solution.py:438
  149.2 1.7 %reshape.48 = bf16[32,2,1920]{2,1,0:T(2,128)(2,1)} reshape(bf16[4,16,1920]{2,1,0:T(8,128)(2,1)} %shard_map.55) | data formatting | bytes 491520 | tf_op jit(solution)/shard_map/reshape | solution.py:473
  (5 shorter events, 0.1 us)
Async XLA Ops:
  0.0 2.0 %copy-start.1 = (bf16[2,15,3,256]{3,0,2,1:T(2,128)(2,1)S(1)}, bf16[2,15,3,256]{3,0,2,1:T(2,128)(2,1)}, u32[]{:S(2)}) copy-start(bf16[2,15,3,256]{3,0,2,1:T(2,128)(2,1)} %param.8) | copy-start | bytes 138244
  2.3 0.7 copy-start.2
  3.0 1.0 copy-start

commit v3 on v2

--- a/solution.py
+++ b/solution.py
@@ -32,8 +32,8 @@
 
 
 def kernel(
-    lat_ref, pad_ref, gain_ref, wloc_ref, out_ref,
-    latp, r1, y1, xq, wz, wf, wos, resid, xn, qkv, pkv, blb, bls, gs, rsb, rst, rso, fo,
+    lat_ref, start_ref, gain_ref, wloc_ref, out_ref,
+    gains, latp, r1, y1, xq, wz, wf, wos, resid, xn, qkv, pkv, blb, bls, gs, rsb, rst, rso, fo,
     az_s, az_r, ay_s, ay_r, wz_s, wz_r, wx_s, wx_r, wy_s, wy_r, wg_s, wg_r,
     wo_s, wo_r, ag_s, ag_r, kv_s, kv_r, bl_s, bl_r, rs_s, rs_r, fi_s, fi_r,
 ):
@@ -85,55 +85,61 @@
     rows_by_z = onehot(col == ((row >> 2) & 3) * 64 + (row >> 4) * 4 + (row & 3))
     chan, pch = iota((480, QP), 0), iota((480, QP), 1)
     spread = onehot((chan == (pch >> 4) * 15 + (pch & 15)) & ((pch & 15) != 15))
-    moved = dot(rows_by_z, lat_ref[...]).astype(BF16)
-    moved = dot(moved, spread) + pad_ref[...]
+    moved = dot_t(rows_by_z, lat_ref[...]).astype(BF16)
+    pad_row = jnp.where((iota((1, QP), 1) & 15) == 15, start_ref[0].astype(F32), 0.0)
+    moved = dot(moved, spread) + pad_row
     latp[...] = moved.astype(BF16).reshape(16, 16, QP)
     wz[0, z] = wloc_ref[0]
     wz[1, z] = wloc_ref[1]
     pl.semaphore_wait(barrier, 15 + 7 + 6 + 4)
 
-    def chain_send(l, d, i):
-        if d == 0:
-            block, to = (z + 17 - i) % 16, dev(x, y, zu, c)
-        else:
-            block, to = (z + i - 1) % 16, dev(x, y, zd, c)
-        send(wz.at[l, block], wz.at[l, block], wz_s.at[l, d, i - 1], wz_r.at[l, d, i - 1], to)
+    reach = (8, 7)
+
+    def chain_send(l, d, block, hop, k):
+        to = dev(x, y, (z + hop) % 16 if d == 0 else (z + 16 - hop) % 16, c)
+        send(wz.at[l, block], wz.at[l, block], wz_s.at[l, d, k - 1], wz_r.at[l, d, k - 1], to)
+
+    def chain_start(l):
+        for k in (1, 2):
+            for d in range(2):
+                chain_send(l, d, z, k, k)
+        scatter_block(l, z, 0)
 
     def chain_step(l, i):
-        arrive(wz.at[l, (z + 16 - i) % 16], wz_r.at[l, 0, i - 1])
-        if i < 8:
-            chain_send(l, 0, i + 1)
-            arrive(wz.at[l, (z + i) % 16], wz_r.at[l, 1, i - 1])
-            if i < 7:
-                chain_send(l, 1, i + 1)
-
-    def scatter_send(l):
-        for a in range(2):
-            half = (x // 2 + a) % 2
-            t = half * 2 + c
-            for b in range(2):
-                j = (c + b) % 2
-                src = wz.at[l, pl.ds(half * 8, 8), j]
-                dst = wf.at[l, y, x]
-                copy = pltpu.make_async_remote_copy(
-                    src_ref=src, dst_ref=dst, send_sem=wx_s.at[l, a * 2 + b], recv_sem=wx_r.at[l, x],
-                    device_id=dev(t, y, z, j), device_id_type=MESH,
-                )
-                if a == 0 and b == 0:
-                    own = pltpu.make_async_copy(src, dst, wx_r.at[l, x])
-
-                    @pl.when(c == x % 2)
-                    def _():
-                        own.start()
-
-                    @pl.when(c != x % 2)
-                    def _():
-                        copy.start()
-
-                    scattered.append(copy)
-                else:
+        for k in (2 * i - 1, 2 * i):
+            for d in range(2):
+                if k <= reach[d]:
+                    block = (z + 16 - k) % 16 if d == 0 else (z + k) % 16
+                    arrive(wz.at[l, block], wz_r.at[l, d, k - 1])
+                    if k + 2 <= reach[d]:
+                        chain_send(l, d, block, 2, k + 2)
+                    scatter_block(l, block, k if d == 0 else 8 + k)
+
+    def scatter_block(l, block, n):
+        half, at = block // 8, block % 8
+        t = half * 2 + c
+        for b in range(2):
+            j = (c + b) % 2
+            src, dst = wz.at[l, block, j], wf.at[l, y, x, at]
+            copy = pltpu.make_async_remote_copy(
+                src_ref=src, dst_ref=dst, send_sem=wx_s.at[l, n, b], recv_sem=wx_r.at[l, x],
+                device_id=dev(t, y, z, j), device_id_type=MESH,
+            )
+            if b == 0:
+                own = pltpu.make_async_copy(src, dst, wx_r.at[l, x])
+
+                @pl.when(t == x)
+                def _():
+                    own.start()
+
+                @pl.when(t != x)
+                def _():
                     copy.start()
-                    sends.append(copy)
+
+                scattered.append((copy, t))
+            else:
+                copy.start()
+                sends.append(copy)
 
     scattered = []
 
@@ -166,8 +172,7 @@
         if part == 1:
             send(wf.at[l, :, :, :, :, pl.ds(384, 128)], wos.at[l], wo_s.at[l], wo_r.at[l], dev(x, y, z, 1 - c))
 
-    chain_send(0, 0, 1)
-    chain_send(0, 1, 1)
+    chain_start(0)
     own_z = pltpu.make_async_copy(latp.at[z], r1.at[z], az_r.at[0])
     own_z.start()
 
@@ -175,14 +180,24 @@
         to = (z + o) % 16
         send(latp.at[to], r1.at[z], az_s.at[o], az_r.at[o], dev(x, y, to, c))
 
-    for i in range(1, 9):
-        latent_send(9 - i)
-        if i > 1:
-            latent_send(7 + i)
+    order = ((8, 7, 9, 6), (10, 5, 11, 4), (12, 3, 13, 2), (14, 1, 15))
+    for i in range(1, 5):
+        for o in order[i - 1]:
+            latent_send(o)
         chain_step(0, i)
-    scatter_send(0)
-    chain_send(1, 0, 1)
-    chain_send(1, 1, 1)
+    rest, split = gain_ref[...], []
+    for _ in range(3):
+        split.append(rest.astype(BF16))
+        rest = rest - split[-1].astype(F32)
+    split = jnp.concatenate(split, axis=0)
+    for q in range(4):
+        base = q * 480 // 128 * 128
+        width = min(640, D - base)
+        chan, pch = iota((width, QP), 0) + (base - q * 480), iota((width, QP), 1)
+        pick = onehot((chan == (pch >> 4) * 15 + (pch & 15)) & ((pch & 15) != 15))
+        parts = dot(split[:, base:base + width], pick)
+        gains[:, q * QP:(q + 1) * QP] = parts[:2] + parts[2:4] + parts[4:]
+    chain_start(1)
 
     own_z.wait()
     for o in range(1, 16):
@@ -217,7 +232,7 @@
         rows = resid[...]
         square = jnp.where(real, rows * rows, 0.0)
         mean_square = jnp.sum(square, axis=1, keepdims=True) * (1.0 / D)
-        normed = jnp.where(real, rows * lax.rsqrt(mean_square + EPSILON) * gain_ref[l], rows)
+        normed = jnp.where(real, rows * lax.rsqrt(mean_square + EPSILON) * gains[l:l + 1], rows)
         xn[l, c, x] = normed.astype(BF16).reshape(4, 16, DP)
 
     low, high = pl.ds(0, 2), pl.ds(2, 2)
@@ -298,18 +313,13 @@
     chain_step(1, 3)
     ring_forward(0, 0, 0)
     gather_forward(0)
-    chain_step(1, 4)
     ring_forward(0, 0, 1)
     gather_sides(0)
-    chain_step(1, 5)
+    chain_step(1, 4)
     ring_forward(0, 0, 2)
     gather_far(0)
-    chain_step(1, 6)
     ring_forward(0, 0, 3)
     ring_send(0, 1)
-    chain_step(1, 7)
-    chain_step(1, 8)
-    scatter_send(1)
     ring_end(0, 0)
 
     for l in range(LAYERS):
@@ -417,9 +427,9 @@
         def _():
             copy.wait_send()
 
-    for copy in scattered:
-
-        @pl.when(c != x % 2)
+    for copy, t in scattered:
+
+        @pl.when(t != x)
         def _():
             copy.wait_send()
 
@@ -428,8 +438,6 @@
 
 
 def local(latent, start_frame, norm_gains, qkv_weight, out_weight):
-    pad_row = jnp.where(jnp.arange(QP) % 16 == 15, start_frame[0].astype(F32), 0.0)[None, :]
-    gains = jnp.pad(norm_gains.reshape(LAYERS, 128, 15), ((0, 0), (0, 0), (0, 1))).reshape(LAYERS, 1, DP)
     both = jnp.concatenate([qkv_weight, out_weight.transpose(0, 2, 1)[:, :, None, :]], axis=2)
     both = both.reshape(LAYERS, 15, 4, 2, 128).transpose(0, 3, 1, 2, 4).reshape(LAYERS, 2, 15, QP)
     both = jnp.pad(both, ((0, 0), (0, 0), (0, 1), (0, 0)))
@@ -438,9 +446,15 @@
     out = pl.pallas_call(
         kernel,
         out_shape=jax.ShapeDtypeStruct((4, 16, D), BF16),
-        in_specs=[pl.BlockSpec(memory_space=vmem)] * 4,
+        in_specs=[
+            pl.BlockSpec(memory_space=vmem),
+            pl.BlockSpec(memory_space=pltpu.SMEM),
+            pl.BlockSpec(memory_space=vmem),
+            pl.BlockSpec(memory_space=vmem),
+        ],
         out_specs=pl.BlockSpec(memory_space=vmem),
         scratch_shapes=[
+            vmem((LAYERS, DP), F32),
             vmem((16, 16, QP), BF16),
             vmem((16, 16, QP), BF16),
             vmem((8, 2, 16, QP), BF16),
@@ -460,7 +474,7 @@
             vmem((LAYERS, 2, 32, DP), BF16),
             vmem((4, 16, D), BF16),
             dma((16,)), dma((16,)), dma((8,)), dma((8,)),
-            dma((LAYERS, 2, 8)), dma((LAYERS, 2, 8)), dma((LAYERS, 4)), dma((LAYERS, 4)),
+            dma((LAYERS, 2, 8)), dma((LAYERS, 2, 8)), dma((LAYERS, 16, 2)), dma((LAYERS, 4)),
             dma((LAYERS, 2, 2, 4)), dma((LAYERS, 2, 2, 4)), dma((LAYERS, 2, 4)), dma((LAYERS, 2, 4)),
             dma((LAYERS,)), dma((LAYERS,)), dma((LAYERS, 11)), dma((LAYERS, 11)),
             dma((LAYERS,)), dma((LAYERS,)), dma((LAYERS,)), dma((LAYERS,)),
@@ -469,7 +483,7 @@
         compiler_params=pltpu.CompilerParams(
             collective_id=0, has_side_effects=True, vmem_limit_bytes=56 * 2**20
         ),
-    )(latent[0], pad_row, gains, both)
+    )(latent[0].T, start_frame, norm_gains, both)
     return out.reshape(32, 2, D)
 
 

time: 151 us -> 144 us (0.954)
  the two profiles are of different devices: /device:TPU:13 before, /device:TPU:5 now
where the time goes in v3:
time: 144 us
  Pallas kernels  140 us (97%)
  local copies, waits for them, and re-layouts  3.32 us (2%)
    pallas_call x1, Pallas kernels, local(): pl.pallas_call(kernel, out_shape=jax.ShapeDtypeStruct((4, 16, D), BF16),...  140 us

profile of v3, /device:TPU:5, one launch (start us, length us, event | category | flops | bytes accessed | tf_op | source)
XLA Modules:
  0.0 144.0 jit_solution(6590832154012872958)
XLA Ops:
  0.0 0.0 copy-start
  0.7 0.8 concatenate.9
  1.4 0.0 copy-done
  1.5 0.1 concatenate.8
  1.6 0.1 maximum_bitcast_fusion
  1.7 0.6 pad.4.wloc_ref
  2.4 139.9 %shard_map.55 = bf16[4,16,1920]{2,1,0:T(8,128)(2,1)} custom-call(bf16[480,256]{1,0:T(8,128)(2,1)} %bitcast.12, s32[1]{0:T(128)S(6)} %copy.11.start_ref, f32[2,1920]{1,0:T(2,128)} %gain_ref.1, bf16[2,2,16,512]{3,2,1,0:T(8,128)(2,1)} %pad.4.wloc_ref), custom_call_target="tpu_custom_call" | custom-call | tf_op jit(solution)/shard_map/pallas_call | solution.py:446
  142.3 1.7 %reshape.11 = bf16[32,2,1920]{2,1,0:T(2,128)(2,1)} reshape(bf16[4,16,1920]{2,1,0:T(8,128)(2,1)} %shard_map.55) | data formatting | bytes 491520 | tf_op jit(solution)/shard_map/reshape | solution.py:487
  (4 shorter events, 0.1 us)
Async XLA Ops:
  0.0 1.5 %copy-start = (bf16[2,15,3,256]{3,0,2,1:T(2,128)(2,1)S(1)}, bf16[2,15,3,256]{3,0,2,1:T(2,128)(2,1)}, u32[]{:S(2)}) copy-start(bf16[2,15,3,256]{3,0,2,1:T(2,128)(2,1)} %param.8) | copy-start | bytes 138244

commit v4 on v3

--- a/solution.py
+++ b/solution.py
@@ -33,7 +33,7 @@
 
 def kernel(
     lat_ref, start_ref, gain_ref, wloc_ref, out_ref,
-    gains, latp, r1, y1, xq, wz, wf, wos, resid, xn, qkv, pkv, blb, bls, gs, rsb, rst, rso, fo,
+    gains, latp, r1, y1, xq, wz, wf, wos, resid, xn, qkv, pkv, blb, bls, gs, rsb, rst, rso, fo, pick,
     az_s, az_r, ay_s, ay_r, wz_s, wz_r, wx_s, wx_r, wy_s, wy_r, wg_s, wg_r,
     wo_s, wo_r, ag_s, ag_r, kv_s, kv_r, bl_s, bl_r, rs_s, rs_r, fi_s, fi_r,
 ):
@@ -194,8 +194,8 @@
         base = q * 480 // 128 * 128
         width = min(640, D - base)
         chan, pch = iota((width, QP), 0) + (base - q * 480), iota((width, QP), 1)
-        pick = onehot((chan == (pch >> 4) * 15 + (pch & 15)) & ((pch & 15) != 15))
-        parts = dot(split[:, base:base + width], pick)
+        chosen = onehot((chan == (pch >> 4) * 15 + (pch & 15)) & ((pch & 15) != 15))
+        parts = dot(split[:, base:base + width], chosen)
         gains[:, q * QP:(q + 1) * QP] = parts[:2] + parts[2:4] + parts[4:]
     chain_start(1)
 
@@ -228,52 +228,58 @@
 
     real = (iota((1, DP), 1) & 15) != 15
 
-    def norm_rows(l):
-        rows = resid[...]
+    def quarter(q):
+        return slice(q * 16, (q + 1) * 16)
+
+    def norm_rows(l, q):
+        rows = resid[quarter(q)]
         square = jnp.where(real, rows * rows, 0.0)
         mean_square = jnp.sum(square, axis=1, keepdims=True) * (1.0 / D)
         normed = jnp.where(real, rows * lax.rsqrt(mean_square + EPSILON) * gains[l:l + 1], rows)
-        xn[l, c, x] = normed.astype(BF16).reshape(4, 16, DP)
-
-    low, high = pl.ds(0, 2), pl.ds(2, 2)
-
-    def gather_copy(l, block, n, to):
-        send(block, block, ag_s.at[l, n], ag_r.at[l, n], to)
-
-    def gather_send(l):
+        xn[l, c, x, q] = normed.astype(BF16)
+
+    def gather_copy(l, block, n, k, to):
+        send(block, block, ag_s.at[l, n, k], ag_r.at[l, n, k], to)
+
+    def gather_send(l, k):
         up, down = dev(xu, y, z, c), dev(xd, y, z, c)
-        gather_copy(l, xn.at[l, c, x, low], 0, up)
-        gather_copy(l, xn.at[l, c, x, high], 1, down)
-        gather_copy(l, xn.at[l, c, x, high], 2, up)
-        gather_copy(l, xn.at[l, c, x, low], 3, down)
-        gather_copy(l, xn.at[l, c, x], 4, dev(x, y, z, 1 - c))
-
-    def gather_forward(l):
-        arrive(xn.at[l, c, xd, low], ag_r.at[l, 0])
-        gather_copy(l, xn.at[l, c, xd, low], 5, dev(xu, y, z, c))
-        arrive(xn.at[l, c, xu, high], ag_r.at[l, 1])
-        gather_copy(l, xn.at[l, c, xu, high], 6, dev(xd, y, z, c))
+        gather_copy(l, xn.at[l, c, x, k], 0, k, up)
+        gather_copy(l, xn.at[l, c, x, 2 + k], 1, k, down)
+        gather_copy(l, xn.at[l, c, x, 2 + k], 2, k, up)
+        gather_copy(l, xn.at[l, c, x, k], 3, k, down)
+        if k == 1:
+            gather_copy(l, xn.at[l, c, x], 4, 0, dev(x, y, z, 1 - c))
+
+    def gather_forward(l, k):
+        arrive(xn.at[l, c, xd, k], ag_r.at[l, 0, k])
+        gather_copy(l, xn.at[l, c, xd, k], 5, k, dev(xu, y, z, c))
+        arrive(xn.at[l, c, xu, 2 + k], ag_r.at[l, 1, k])
+        gather_copy(l, xn.at[l, c, xu, 2 + k], 6, k, dev(xd, y, z, c))
 
     def gather_sides(l):
         sibling = dev(x, y, z, 1 - c)
-        arrive(xn.at[l, c, xd, high], ag_r.at[l, 2])
-        gather_copy(l, xn.at[l, c, xd], 7, sibling)
-        arrive(xn.at[l, c, xu, low], ag_r.at[l, 3])
-        gather_copy(l, xn.at[l, c, xu], 8, sibling)
+        for k in range(2):
+            arrive(xn.at[l, c, xd, 2 + k], ag_r.at[l, 2, k])
+        gather_copy(l, xn.at[l, c, xd], 7, 0, sibling)
+        for k in range(2):
+            arrive(xn.at[l, c, xu, k], ag_r.at[l, 3, k])
+        gather_copy(l, xn.at[l, c, xu], 8, 0, sibling)
 
     def gather_far(l):
         sibling = dev(x, y, z, 1 - c)
-        arrive(xn.at[l, c, xo, low], ag_r.at[l, 5])
-        gather_copy(l, xn.at[l, c, xo, low], 9, sibling)
-        arrive(xn.at[l, c, xo, high], ag_r.at[l, 6])
-        gather_copy(l, xn.at[l, c, xo, high], 10, sibling)
+        for k in range(2):
+            arrive(xn.at[l, c, xo, k], ag_r.at[l, 5, k])
+            gather_copy(l, xn.at[l, c, xo, k], 9, k, sibling)
+            arrive(xn.at[l, c, xo, 2 + k], ag_r.at[l, 6, k])
+            gather_copy(l, xn.at[l, c, xo, 2 + k], 10, k, sibling)
 
     def gather_end(l):
-        arrive(xn.at[l, 1 - c, x], ag_r.at[l, 4])
-        arrive(xn.at[l, 1 - c, xd], ag_r.at[l, 7])
-        arrive(xn.at[l, 1 - c, xu], ag_r.at[l, 8])
-        arrive(xn.at[l, 1 - c, xo, low], ag_r.at[l, 9])
-        arrive(xn.at[l, 1 - c, xo, high], ag_r.at[l, 10])
+        arrive(xn.at[l, 1 - c, x], ag_r.at[l, 4, 0])
+        arrive(xn.at[l, 1 - c, xd], ag_r.at[l, 7, 0])
+        arrive(xn.at[l, 1 - c, xu], ag_r.at[l, 8, 0])
+        for k in range(2):
+            arrive(xn.at[l, 1 - c, xo, k], ag_r.at[l, 9, k])
+            arrive(xn.at[l, 1 - c, xo, 2 + k], ag_r.at[l, 10, k])
 
     def project(l):
         weight = wf[l, :, :, :, :, :384].reshape(DP, 384)
@@ -308,11 +314,14 @@
         return jnp.where(lane < 64, parts[0], parts[1]).astype(BF16)
 
     gather_like = pl.ds(128, 256)
-    norm_rows(0)
-    gather_send(0)
+    for k in range(2):
+        norm_rows(0, k)
+        norm_rows(0, 2 + k)
+        gather_send(0, k)
     chain_step(1, 3)
+    gather_forward(0, 0)
     ring_forward(0, 0, 0)
-    gather_forward(0)
+    gather_forward(0, 1)
     ring_forward(0, 0, 1)
     gather_sides(0)
     chain_step(1, 4)
@@ -322,6 +331,47 @@
     ring_send(0, 1)
     ring_end(0, 0)
 
+    def drop_pads():
+        for b in range(D // 128):
+            first, width = window(b)
+            a, ch = iota((width, 128), 0) + first, iota((width, 128), 1) + b * 128
+            group = (ch * 4370) >> 16
+            pick[b, :width] = onehot(a == group * 16 + (ch - group * 15))
+
+    def window(b):
+        first = ((b * 128 // 15) * 16 + (b * 128) % 15) // 128 * 128
+        return first, min(384, DP - first)
+
+    last = []
+    stretch = pair * 2 + c
+
+    def finish(k):
+        refined = jnp.concatenate([resid[quarter(k)], resid[quarter(2 + k)]], axis=0).astype(BF16)
+        for b in range(D // 128):
+            first, width = window(b)
+            packed = dot(refined[:, first:first + width], pick[b, :width]).astype(BF16)
+            fo[k, :, b * 128:(b + 1) * 128] = packed[:16]
+            fo[2 + k, :, b * 128:(b + 1) * 128] = packed[16:]
+        for q in (k, 2 + k):
+            to_z = stretch + 8 * (q // 2)
+            copy = pltpu.make_async_remote_copy(
+                src_ref=fo.at[q], dst_ref=out_ref.at[x], send_sem=fi_s.at[q], recv_sem=fi_r.at[x],
+                device_id=dev(clip_x, y, to_z, q % 2), device_id_type=MESH,
+            )
+            own = pltpu.make_async_copy(fo.at[q], out_ref.at[x], fi_r.at[x])
+            here = (clip_x == x) & (to_z == z) & (c == q % 2)
+            last.append((copy, here))
+            launch(copy, own, here)
+
+    def launch(copy, own, here):
+        @pl.when(here)
+        def _():
+            own.start()
+
+        @pl.when(jnp.logical_not(here))
+        def _():
+            copy.start()
+
     for l in range(LAYERS):
         project(l)
         send(qkv.at[1, :, gather_like], pkv.at[l], kv_s.at[l], kv_r.at[l], dev(x, y, zu, c))
@@ -329,110 +379,95 @@
             starts = [first_frame(p) for p in range(2)]
         see = frame.astype(F32) >= starts[1]
         blb[1] = attend(1, qkv[0, :, 128:256], qkv[0, :, 256:384], see).reshape(4, 64, 128)
+        for p in range(4):
+            ring_forward(l, 1, p)
         if l == 0:
-            for p in range(4):
-                ring_forward(0, 1, p)
             ring_send(1, 0)
+            drop_pads()
         arrive(pkv.at[l], kv_r.at[l])
         see = (frame.astype(F32) >= starts[0]) & (pair > 0)
         blb[0] = attend(0, pkv[l, :, :128], pkv[l, :, 128:], see).reshape(4, 64, 128)
         send(blb.at[1 - c], bls.at[l], bl_s.at[l], bl_r.at[l], dev(x, y, z, 1 - c))
-        if l == 0:
-            ring_end(0, 1)
+        ring_end(l, 1)
         arrive(bls.at[l], bl_r.at[l])
         arrive(wos.at[l], wo_r.at[l])
         weight = jnp.concatenate([wf[l, :, :, :, :, 384:], wos[l]], axis=4).reshape(DP, 256)
 
         def update(to):
             blended = jnp.concatenate([blb[c, to], bls[l, to]], axis=1)
-            gs[l, to] = dot_t(blended, weight).astype(BF16)
+            gs[l, to] = dot_t(blended, weight).astype(BF16).reshape(4, 16, DP)
 
         up, down = dev(xu, y, z, c), dev(xd, y, z, c)
-        first, second = pl.ds(0, 32), pl.ds(32, 32)
-
-        def scatter_copy(src, dst, n, to):
-            send(src, dst, rs_s.at[l, n], rs_r.at[l, n], to)
+
+        def scatter_copy(src, dst, n, k, to):
+            send(src, dst, rs_s.at[l, n, k], rs_r.at[l, n, k], to)
+
+        def scatter_plain(k):
+            scatter_copy(gs.at[l, xu, 2 + k], rsb.at[l, 0, 2 + k], 2, k, up)
+            scatter_copy(gs.at[l, xd, k], rsb.at[l, 1, k], 3, k, down)
+
+        def scatter_sum(k):
+            arrive(rst.at[l, 0, k], rs_r.at[l, 0, k])
+            rso[l, 0, k] = (gs[l, xu, k].astype(F32) + rst[l, 0, k].astype(F32)).astype(BF16)
+            scatter_copy(rso.at[l, 0, k], rsb.at[l, 0, k], 4, k, up)
+            arrive(rst.at[l, 1, k], rs_r.at[l, 1, k])
+            rso[l, 1, k] = (gs[l, xd, 2 + k].astype(F32) + rst[l, 1, k].astype(F32)).astype(BF16)
+            scatter_copy(rso.at[l, 1, k], rsb.at[l, 1, 2 + k], 5, k, down)
 
         update(xo)
-        scatter_copy(gs.at[l, xo, first], rst.at[l, 0], 0, up)
-        scatter_copy(gs.at[l, xo, second], rst.at[l, 1], 1, down)
+        for k in range(2):
+            scatter_copy(gs.at[l, xo, k], rst.at[l, 0, k], 0, k, up)
+            scatter_copy(gs.at[l, xo, 2 + k], rst.at[l, 1, k], 1, k, down)
         update(xu)
-        scatter_copy(gs.at[l, xu, second], rsb.at[l, 0, second], 2, up)
         update(xd)
-        scatter_copy(gs.at[l, xd, first], rsb.at[l, 1, first], 3, down)
-        arrive(rst.at[l, 0], rs_r.at[l, 0])
-        rso[l, 0] = (gs[l, xu, :32].astype(F32) + rst[l, 0].astype(F32)).astype(BF16)
-        scatter_copy(rso.at[l, 0], rsb.at[l, 0, first], 4, up)
-        arrive(rst.at[l, 1], rs_r.at[l, 1])
-        rso[l, 1] = (gs[l, xd, 32:].astype(F32) + rst[l, 1].astype(F32)).astype(BF16)
-        scatter_copy(rso.at[l, 1], rsb.at[l, 1, second], 5, down)
+        scatter_plain(0)
+        scatter_sum(0)
+        scatter_plain(1)
+        scatter_sum(1)
         update(x)
         if l == 0:
-            for p in range(4):
-                ring_forward(1, 0, p)
+            ring_forward(1, 0, 0)
+            ring_forward(1, 0, 1)
+        drain_upto = len(sends)
+        for k in range(2):
+            arrive(rsb.at[l, 0, 2 + k], rs_r.at[l, 2, k])
+            arrive(rsb.at[l, 1, k], rs_r.at[l, 3, k])
+            arrive(rsb.at[l, 0, k], rs_r.at[l, 4, k])
+            arrive(rsb.at[l, 1, 2 + k], rs_r.at[l, 5, k])
+            for q in (k, 2 + k):
+                total = gs[l, x, q].astype(F32) + rsb[l, 0, q].astype(F32) + rsb[l, 1, q].astype(F32)
+                resid[quarter(q)] += total
+                if l == 0:
+                    norm_rows(1, q)
+            if l == 0:
+                gather_send(1, k)
+            else:
+                finish(k)
+        if l == 0:
+            gather_forward(1, 0)
+            ring_forward(1, 0, 2)
+            ring_forward(1, 0, 3)
+            gather_forward(1, 1)
             ring_send(1, 1)
-        arrive(rsb.at[l, 0, second], rs_r.at[l, 2])
-        arrive(rsb.at[l, 1, first], rs_r.at[l, 3])
-        arrive(rsb.at[l, 0, first], rs_r.at[l, 4])
-        arrive(rsb.at[l, 1, second], rs_r.at[l, 5])
-        resid[...] += gs[l, x].astype(F32) + rsb[l, 0].astype(F32) + rsb[l, 1].astype(F32)
-        if l == 0:
-            norm_rows(1)
-            gather_send(1)
-            drain_upto = len(sends)
-            gather_forward(1)
             gather_sides(1)
             for copy in sends[:drain_upto]:
                 copy.wait_send()
             del sends[:drain_upto]
             gather_far(1)
-            for p in range(4):
-                ring_forward(1, 1, p)
             ring_end(1, 0)
-            ring_end(1, 1)
-
-    refined = resid[...].astype(BF16)
-    for b in range(D // 128):
-        first = ((b * 128 // 15) * 16 + (b * 128) % 15) // 128 * 128
-        width = min(384, DP - first)
-        a, ch = iota((width, 128), 0) + first, iota((width, 128), 1) + b * 128
-        group = (ch * 4370) >> 16
-        pick = onehot(a == group * 16 + (ch - group * 15))
-        fo[:, :, b * 128:(b + 1) * 128] = dot(refined[:, first:first + width], pick).astype(BF16).reshape(4, 16, 128)
-    last = []
-    stretch = pair * 2 + c
-    for q in range(4):
-        to_z = stretch + 8 * (q // 2)
-        copy = pltpu.make_async_remote_copy(
-            src_ref=fo.at[q], dst_ref=out_ref.at[x], send_sem=fi_s.at[q], recv_sem=fi_r.at[x],
-            device_id=dev(clip_x, y, to_z, q % 2), device_id_type=MESH,
-        )
-        own = pltpu.make_async_copy(fo.at[q], out_ref.at[x], fi_r.at[x])
-        here = (clip_x == x) & (to_z == z) & (c == q % 2)
-        last.append((copy, here))
-
-        @pl.when(here)
-        def _():
-            own.start()
-
-        @pl.when(jnp.logical_not(here))
-        def _():
-            copy.start()
 
     for p in range(4):
         arrive(out_ref.at[p], fi_r.at[p])
-    for copy, here in last:
-
-        @pl.when(jnp.logical_not(here))
+
+    def settle(copy, there):
+        @pl.when(there)
         def _():
             copy.wait_send()
 
+    for copy, here in last:
+        settle(copy, jnp.logical_not(here))
     for copy, t in scattered:
-
-        @pl.when(t != x)
-        def _():
-            copy.wait_send()
-
+        settle(copy, t != x)
     for copy in sends:
         copy.wait_send()
 
@@ -468,17 +503,18 @@
             vmem((LAYERS, 256, 256), BF16),
             vmem((2, 4, 64, 128), BF16),
             vmem((LAYERS, 4, 64, 128), BF16),
-            vmem((LAYERS, 4, 64, DP), BF16),
-            vmem((LAYERS, 2, 64, DP), BF16),
-            vmem((LAYERS, 2, 32, DP), BF16),
-            vmem((LAYERS, 2, 32, DP), BF16),
+            vmem((LAYERS, 4, 4, 16, DP), BF16),
+            vmem((LAYERS, 2, 4, 16, DP), BF16),
+            vmem((LAYERS, 2, 2, 16, DP), BF16),
+            vmem((LAYERS, 2, 2, 16, DP), BF16),
             vmem((4, 16, D), BF16),
+            vmem((D // 128, 384, 128), BF16),
             dma((16,)), dma((16,)), dma((8,)), dma((8,)),
             dma((LAYERS, 2, 8)), dma((LAYERS, 2, 8)), dma((LAYERS, 16, 2)), dma((LAYERS, 4)),
             dma((LAYERS, 2, 2, 4)), dma((LAYERS, 2, 2, 4)), dma((LAYERS, 2, 4)), dma((LAYERS, 2, 4)),
-            dma((LAYERS,)), dma((LAYERS,)), dma((LAYERS, 11)), dma((LAYERS, 11)),
+            dma((LAYERS,)), dma((LAYERS,)), dma((LAYERS, 11, 2)), dma((LAYERS, 11, 2)),
             dma((LAYERS,)), dma((LAYERS,)), dma((LAYERS,)), dma((LAYERS,)),
-            dma((LAYERS, 6)), dma((LAYERS, 6)), dma((4,)), dma((4,)),
+            dma((LAYERS, 6, 2)), dma((LAYERS, 6, 2)), dma((4,)), dma((4,)),
         ],
         compiler_params=pltpu.CompilerParams(
             collective_id=0, has_side_effects=True, vmem_limit_bytes=56 * 2**20

time: 144 us -> 140 us (0.972)
  Pallas kernels: 140 us -> 136 us
    pallas_call x1, Pallas kernels: 140 us -> 136 us  [local(): pl.pallas_call(kernel, out_shape=jax.ShapeDtypeStruct((4, 16, D), BF16),...]
where the time goes in v4:
time: 140 us
  Pallas kernels  136 us (97%)
  local copies, waits for them, and re-layouts  3.32 us (2%)
    pallas_call x1, Pallas kernels, local(): pl.pallas_call(kernel, out_shape=jax.ShapeDtypeStruct((4, 16, D), BF16),...  136 us

profile of v4, /device:TPU:5, one launch (start us, length us, event | category | flops | bytes accessed | tf_op | source)
XLA Modules:
  0.0 140.0 jit_solution(7557323989427556267)
XLA Ops:
  0.0 0.0 copy-start
  0.7 0.8 concatenate.9
  1.4 0.0 copy-done
  1.5 0.1 concatenate.8
  1.6 0.1 maximum_bitcast_fusion
  1.7 0.6 pad.4.wloc_ref
  2.4 135.9 %shard_map.55 = bf16[4,16,1920]{2,1,0:T(8,128)(2,1)} custom-call(bf16[480,256]{1,0:T(8,128)(2,1)} %bitcast.12, s32[1]{0:T(128)S(6)} %copy.11.start_ref, f32[2,1920]{1,0:T(2,128)} %gain_ref.1, bf16[2,2,16,512]{3,2,1,0:T(8,128)(2,1)} %pad.4.wloc_ref), custom_call_target="tpu_custom_call" | custom-call | tf_op jit(solution)/shard_map/pallas_call | solution.py:481
  138.3 1.7 %reshape.11 = bf16[32,2,1920]{2,1,0:T(2,128)(2,1)} reshape(bf16[4,16,1920]{2,1,0:T(8,128)(2,1)} %shard_map.55) | data formatting | bytes 491520 | tf_op jit(solution)/shard_map/reshape | solution.py:523
  (4 shorter events, 0.1 us)
Async XLA Ops:
  0.0 1.5 %copy-start = (bf16[2,15,3,256]{3,0,2,1:T(2,128)(2,1)S(1)}, bf16[2,15,3,256]{3,0,2,1:T(2,128)(2,1)}, u32[]{:S(2)}) copy-start(bf16[2,15,3,256]{3,0,2,1:T(2,128)(2,1)} %param.8) | copy-start | bytes 138244

commit v5 on v4

--- a/solution.py
+++ b/solution.py
@@ -79,16 +79,8 @@
         for j in range(2):
             greet(dev(x, (y + o) % 4, z, (c + j) % 2))
     for o in range(4):
-        greet(dev((x + o) % 4, y, x * 4 + zl // 2, zl % 2))
-
-    row, col = iota((256, 256), 0), iota((256, 256), 1)
-    rows_by_z = onehot(col == ((row >> 2) & 3) * 64 + (row >> 4) * 4 + (row & 3))
-    chan, pch = iota((480, QP), 0), iota((480, QP), 1)
-    spread = onehot((chan == (pch >> 4) * 15 + (pch & 15)) & ((pch & 15) != 15))
-    moved = dot_t(rows_by_z, lat_ref[...]).astype(BF16)
-    pad_row = jnp.where((iota((1, QP), 1) & 15) == 15, start_ref[0].astype(F32), 0.0)
-    moved = dot(moved, spread) + pad_row
-    latp[...] = moved.astype(BF16).reshape(16, 16, QP)
+        greet(dev((x + o) % 4, y, x * 4 + zl // 2, zh))
+
     wz[0, z] = wloc_ref[0]
     wz[1, z] = wloc_ref[1]
     pl.semaphore_wait(barrier, 15 + 7 + 6 + 4)
@@ -173,6 +165,16 @@
             send(wf.at[l, :, :, :, :, pl.ds(384, 128)], wos.at[l], wo_s.at[l], wo_r.at[l], dev(x, y, z, 1 - c))
 
     chain_start(0)
+
+    row, col = iota((256, 256), 0), iota((256, 256), 1)
+    rows_by_z = onehot(col == ((row >> 2) & 3) * 64 + (row >> 4) * 4 + (row & 3))
+    chan, pch = iota((480, QP), 0), iota((480, QP), 1)
+    spread = onehot((chan == (pch >> 4) * 15 + (pch & 15)) & ((pch & 15) != 15))
+    moved = dot_t(rows_by_z, lat_ref[...]).astype(BF16)
+    pad_row = jnp.where((iota((1, QP), 1) & 15) == 15, start_ref[0].astype(F32), 0.0)
+    moved = dot(moved, spread) + pad_row
+    latp[...] = moved.astype(BF16).reshape(16, 16, QP)
+
     own_z = pltpu.make_async_copy(latp.at[z], r1.at[z], az_r.at[0])
     own_z.start()
 
@@ -197,95 +199,99 @@
         chosen = onehot((chan == (pch >> 4) * 15 + (pch & 15)) & ((pch & 15) != 15))
         parts = dot(split[:, base:base + width], chosen)
         gains[:, q * QP:(q + 1) * QP] = parts[:2] + parts[2:4] + parts[4:]
-    chain_start(1)
 
     own_z.wait()
     for o in range(1, 16):
         arrive(r1.at[(z + 16 - o) % 16], az_r.at[o])
     rows_by_y = onehot(col == ((row >> 1) & 15) * 16 + (row >> 5) * 2 + (row & 1))
     y1[...] = dot(rows_by_y, r1[...].reshape(256, QP)).astype(BF16).reshape(8, 2, 16, QP)
-    own_y = pltpu.make_async_copy(y1.at[y * 2 + c], xq.at[:, c, y], ay_r.at[0])
-    own_y.start()
-    for o in range(4):
-        for j in range(2):
-            if o or j:
-                to, par = (y + o) % 4, (c + j) % 2
-                send(
-                    y1.at[to * 2 + par], xq.at[:, c, y], ay_s.at[o * 2 + j], ay_r.at[o * 2 + j],
-                    dev(x, to, z, par),
-                )
+    def latent_pass(o, par):
+        to = (y + o) % 4
+        return pltpu.make_async_remote_copy(
+            src_ref=y1.at[to * 2 + par], dst_ref=xq.at[:, c, par, y % 2],
+            send_sem=ay_s.at[o, par], recv_sem=ay_r.at[par, y % 2, c],
+            device_id=dev(x, to, z, y // 2), device_id_type=MESH,
+        )
+
+    for par in (1, 0):
+        for o in (1, 3, 2):
+            copy = latent_pass(o, par)
+            copy.start()
+            sends.append(copy)
+
+        @pl.when(c == y // 2)
+        def _():
+            pltpu.make_async_copy(y1.at[y * 2 + par], xq.at[:, c, par, y % 2], ay_r.at[par, y % 2, c]).start()
+
+        @pl.when(c != y // 2)
+        def _():
+            latent_pass(0, par).start()
+
+    chain_start(1)
+    ring_send(0, 0)
     chain_step(1, 1)
-    ring_send(0, 0)
-    chain_step(1, 2)
-
-    own_y.wait()
-    for o in range(4):
-        for j in range(2):
-            if o or j:
-                arrive(xq.at[:, (c + j) % 2, (y + 4 - o) % 4], ay_r.at[o * 2 + j])
+
+    for par in range(2):
+        for e in range(2):
+            for j in range(2):
+                arrive(xq.at[:, j, par, e], ay_r.at[par, e, j])
     for h in range(4):
         resid[:, h * QP:(h + 1) * QP] = xq[h // 2, h % 2].reshape(64, QP).astype(F32)
 
     real = (iota((1, DP), 1) & 15) != 15
 
-    def quarter(q):
-        return slice(q * 16, (q + 1) * 16)
-
-    def norm_rows(l, q):
-        rows = resid[quarter(q)]
+    def slot(k, e):
+        return slice((k * 2 + e) * 16, (k * 2 + e + 1) * 16)
+
+    def norm_rows(l, k, e):
+        rows = resid[slot(k, e)]
         square = jnp.where(real, rows * rows, 0.0)
         mean_square = jnp.sum(square, axis=1, keepdims=True) * (1.0 / D)
         normed = jnp.where(real, rows * lax.rsqrt(mean_square + EPSILON) * gains[l:l + 1], rows)
-        xn[l, c, x, q] = normed.astype(BF16)
+        xn[l, k, x, c * 2 + e] = normed.astype(BF16)
+
+    def rows_of(l, k, xx, e):
+        return xn.at[l, k, xx, c * 2 + e]
+
+    def both_of(l, k, xx, cc):
+        return xn.at[l, k, xx, pl.ds(cc * 2, 2)]
 
     def gather_copy(l, block, n, k, to):
         send(block, block, ag_s.at[l, n, k], ag_r.at[l, n, k], to)
 
     def gather_send(l, k):
         up, down = dev(xu, y, z, c), dev(xd, y, z, c)
-        gather_copy(l, xn.at[l, c, x, k], 0, k, up)
-        gather_copy(l, xn.at[l, c, x, 2 + k], 1, k, down)
-        gather_copy(l, xn.at[l, c, x, 2 + k], 2, k, up)
-        gather_copy(l, xn.at[l, c, x, k], 3, k, down)
-        if k == 1:
-            gather_copy(l, xn.at[l, c, x], 4, 0, dev(x, y, z, 1 - c))
+        gather_copy(l, rows_of(l, k, x, 0), 0, k, up)
+        gather_copy(l, rows_of(l, k, x, 1), 1, k, down)
+        gather_copy(l, rows_of(l, k, x, 1), 2, k, up)
+        gather_copy(l, rows_of(l, k, x, 0), 3, k, down)
+        gather_copy(l, both_of(l, k, x, c), 4, k, dev(x, y, z, 1 - c))
 
     def gather_forward(l, k):
-        arrive(xn.at[l, c, xd, k], ag_r.at[l, 0, k])
-        gather_copy(l, xn.at[l, c, xd, k], 5, k, dev(xu, y, z, c))
-        arrive(xn.at[l, c, xu, 2 + k], ag_r.at[l, 1, k])
-        gather_copy(l, xn.at[l, c, xu, 2 + k], 6, k, dev(xd, y, z, c))
-
-    def gather_sides(l):
+        arrive(rows_of(l, k, xd, 0), ag_r.at[l, 0, k])
+        gather_copy(l, rows_of(l, k, xd, 0), 5, k, dev(xu, y, z, c))
+        arrive(rows_of(l, k, xu, 1), ag_r.at[l, 1, k])
+        gather_copy(l, rows_of(l, k, xu, 1), 6, k, dev(xd, y, z, c))
+
+    def gather_sides(l, k):
         sibling = dev(x, y, z, 1 - c)
-        for k in range(2):
-            arrive(xn.at[l, c, xd, 2 + k], ag_r.at[l, 2, k])
-        gather_copy(l, xn.at[l, c, xd], 7, 0, sibling)
-        for k in range(2):
-            arrive(xn.at[l, c, xu, k], ag_r.at[l, 3, k])
-        gather_copy(l, xn.at[l, c, xu], 8, 0, sibling)
-
-    def gather_far(l):
-        sibling = dev(x, y, z, 1 - c)
-        for k in range(2):
-            arrive(xn.at[l, c, xo, k], ag_r.at[l, 5, k])
-            gather_copy(l, xn.at[l, c, xo, k], 9, k, sibling)
-            arrive(xn.at[l, c, xo, 2 + k], ag_r.at[l, 6, k])
-            gather_copy(l, xn.at[l, c, xo, 2 + k], 10, k, sibling)
-
-    def gather_end(l):
-        arrive(xn.at[l, 1 - c, x], ag_r.at[l, 4, 0])
-        arrive(xn.at[l, 1 - c, xd], ag_r.at[l, 7, 0])
-        arrive(xn.at[l, 1 - c, xu], ag_r.at[l, 8, 0])
-        for k in range(2):
-            arrive(xn.at[l, 1 - c, xo, k], ag_r.at[l, 9, k])
-            arrive(xn.at[l, 1 - c, xo, 2 + k], ag_r.at[l, 10, k])
-
-    def project(l):
+        arrive(rows_of(l, k, xd, 1), ag_r.at[l, 2, k])
+        gather_copy(l, both_of(l, k, xd, c), 7, k, sibling)
+        arrive(rows_of(l, k, xu, 0), ag_r.at[l, 3, k])
+        gather_copy(l, both_of(l, k, xu, c), 8, k, sibling)
+
+    def gather_far(l, k):
+        arrive(rows_of(l, k, xo, 0), ag_r.at[l, 5, k])
+        arrive(rows_of(l, k, xo, 1), ag_r.at[l, 6, k])
+        gather_copy(l, both_of(l, k, xo, c), 9, k, dev(x, y, z, 1 - c))
+
+    def gather_end(l, k):
+        for xx, n in ((x, 4), (xd, 7), (xu, 8), (xo, 9)):
+            arrive(both_of(l, k, xx, 1 - c), ag_r.at[l, n, k])
+
+    def project(l, k):
         weight = wf[l, :, :, :, :, :384].reshape(DP, 384)
-        qkv[c] = dot(xn[l, c].reshape(256, DP), weight).astype(BF16)
-        gather_end(l)
-        qkv[1 - c] = dot(xn[l, 1 - c].reshape(256, DP), weight).astype(BF16)
+        qkv[k] = dot(xn[l, k].reshape(256, DP), weight).astype(BF16)
 
     lane = iota((1, 128), 1)
     frame = iota((1, 256), 1) & 1
@@ -314,21 +320,24 @@
         return jnp.where(lane < 64, parts[0], parts[1]).astype(BF16)
 
     gather_like = pl.ds(128, 256)
-    for k in range(2):
-        norm_rows(0, k)
-        norm_rows(0, 2 + k)
+    for k in (1, 0):
+        norm_rows(0, k, 0)
+        norm_rows(0, k, 1)
         gather_send(0, k)
+    chain_step(1, 2)
+    gather_forward(0, 1)
+    ring_forward(0, 0, 0)
+    gather_forward(0, 0)
+    ring_forward(0, 0, 1)
+    gather_sides(0, 1)
+    gather_sides(0, 0)
     chain_step(1, 3)
-    gather_forward(0, 0)
-    ring_forward(0, 0, 0)
-    gather_forward(0, 1)
-    ring_forward(0, 0, 1)
-    gather_sides(0)
-    chain_step(1, 4)
     ring_forward(0, 0, 2)
-    gather_far(0)
+    gather_far(0, 1)
+    gather_far(0, 0)
     ring_forward(0, 0, 3)
     ring_send(0, 1)
+    chain_step(1, 4)
     ring_end(0, 0)
 
     def drop_pads():
@@ -343,23 +352,21 @@
         return first, min(384, DP - first)
 
     last = []
-    stretch = pair * 2 + c
 
     def finish(k):
-        refined = jnp.concatenate([resid[quarter(k)], resid[quarter(2 + k)]], axis=0).astype(BF16)
+        refined = resid[k * 32:(k + 1) * 32].astype(BF16)
         for b in range(D // 128):
             first, width = window(b)
             packed = dot(refined[:, first:first + width], pick[b, :width]).astype(BF16)
-            fo[k, :, b * 128:(b + 1) * 128] = packed[:16]
-            fo[2 + k, :, b * 128:(b + 1) * 128] = packed[16:]
-        for q in (k, 2 + k):
-            to_z = stretch + 8 * (q // 2)
+            fo[k, :, :, b * 128:(b + 1) * 128] = packed.reshape(2, 16, 128)
+        to_z = pair * 2 + k + 8 * c
+        for e in range(2):
             copy = pltpu.make_async_remote_copy(
-                src_ref=fo.at[q], dst_ref=out_ref.at[x], send_sem=fi_s.at[q], recv_sem=fi_r.at[x],
-                device_id=dev(clip_x, y, to_z, q % 2), device_id_type=MESH,
+                src_ref=fo.at[k, e], dst_ref=out_ref.at[x], send_sem=fi_s.at[k, e], recv_sem=fi_r.at[x],
+                device_id=dev(clip_x, y, to_z, e), device_id_type=MESH,
             )
-            own = pltpu.make_async_copy(fo.at[q], out_ref.at[x], fi_r.at[x])
-            here = (clip_x == x) & (to_z == z) & (c == q % 2)
+            own = pltpu.make_async_copy(fo.at[k, e], out_ref.at[x], fi_r.at[x])
+            here = (clip_x == x) & (to_z == z) & (c == e)
             last.append((copy, here))
             launch(copy, own, here)
 
@@ -373,12 +380,24 @@
             copy.start()
 
     for l in range(LAYERS):
-        project(l)
+        gather_end(l, 1)
+        project(l, 1)
         send(qkv.at[1, :, gather_like], pkv.at[l], kv_s.at[l], kv_r.at[l], dev(x, y, zu, c))
+        if l == 1:
+            gather_sides(l, 0)
+            gather_far(l, 0)
+        gather_end(l, 0)
+        project(l, 0)
         if l == 0:
             starts = [first_frame(p) for p in range(2)]
+
+        def pass_blended(p):
+            theirs = blb.at[p, :, pl.ds((1 - c) * 2, 2)]
+            send(theirs, bls.at[l, p], bl_s.at[l, p], bl_r.at[l, p], dev(x, y, z, 1 - c))
+
         see = frame.astype(F32) >= starts[1]
-        blb[1] = attend(1, qkv[0, :, 128:256], qkv[0, :, 256:384], see).reshape(4, 64, 128)
+        blb[1] = attend(1, qkv[0, :, 128:256], qkv[0, :, 256:384], see).reshape(4, 4, 16, 128)
+        pass_blended(1)
         for p in range(4):
             ring_forward(l, 1, p)
         if l == 0:
@@ -386,74 +405,76 @@
             drop_pads()
         arrive(pkv.at[l], kv_r.at[l])
         see = (frame.astype(F32) >= starts[0]) & (pair > 0)
-        blb[0] = attend(0, pkv[l, :, :128], pkv[l, :, 128:], see).reshape(4, 64, 128)
-        send(blb.at[1 - c], bls.at[l], bl_s.at[l], bl_r.at[l], dev(x, y, z, 1 - c))
+        blb[0] = attend(0, pkv[l, :, :128], pkv[l, :, 128:], see).reshape(4, 4, 16, 128)
+        pass_blended(0)
         ring_end(l, 1)
-        arrive(bls.at[l], bl_r.at[l])
         arrive(wos.at[l], wo_r.at[l])
         weight = jnp.concatenate([wf[l, :, :, :, :, 384:], wos[l]], axis=4).reshape(DP, 256)
 
-        def update(to):
-            blended = jnp.concatenate([blb[c, to], bls[l, to]], axis=1)
-            gs[l, to] = dot_t(blended, weight).astype(BF16).reshape(4, 16, DP)
+        def update(k):
+            arrive(bls.at[l, k], bl_r.at[l, k])
+            mine = blb[k, :, pl.ds(c * 2, 2)].reshape(128, 128)
+            blended = jnp.concatenate([mine, bls[l, k].reshape(128, 128)], axis=1)
+            gs[l, k] = dot_t(blended, weight).astype(BF16).reshape(4, 2, 16, DP)
 
         up, down = dev(xu, y, z, c), dev(xd, y, z, c)
 
         def scatter_copy(src, dst, n, k, to):
             send(src, dst, rs_s.at[l, n, k], rs_r.at[l, n, k], to)
 
+        def scatter_far(k):
+            scatter_copy(gs.at[l, k, xo, 0], rst.at[l, 0, k], 0, k, up)
+            scatter_copy(gs.at[l, k, xo, 1], rst.at[l, 1, k], 1, k, down)
+
         def scatter_plain(k):
-            scatter_copy(gs.at[l, xu, 2 + k], rsb.at[l, 0, 2 + k], 2, k, up)
-            scatter_copy(gs.at[l, xd, k], rsb.at[l, 1, k], 3, k, down)
+            scatter_copy(gs.at[l, k, xu, 1], rsb.at[l, 0, k, 1], 2, k, up)
+            scatter_copy(gs.at[l, k, xd, 0], rsb.at[l, 1, k, 0], 3, k, down)
 
         def scatter_sum(k):
             arrive(rst.at[l, 0, k], rs_r.at[l, 0, k])
-            rso[l, 0, k] = (gs[l, xu, k].astype(F32) + rst[l, 0, k].astype(F32)).astype(BF16)
-            scatter_copy(rso.at[l, 0, k], rsb.at[l, 0, k], 4, k, up)
+            rso[l, 0, k] = (gs[l, k, xu, 0].astype(F32) + rst[l, 0, k].astype(F32)).astype(BF16)
+            scatter_copy(rso.at[l, 0, k], rsb.at[l, 0, k, 0], 4, k, up)
             arrive(rst.at[l, 1, k], rs_r.at[l, 1, k])
-            rso[l, 1, k] = (gs[l, xd, 2 + k].astype(F32) + rst[l, 1, k].astype(F32)).astype(BF16)
-            scatter_copy(rso.at[l, 1, k], rsb.at[l, 1, 2 + k], 5, k, down)
-
-        update(xo)
-        for k in range(2):
-            scatter_copy(gs.at[l, xo, k], rst.at[l, 0, k], 0, k, up)
-            scatter_copy(gs.at[l, xo, 2 + k], rst.at[l, 1, k], 1, k, down)
-        update(xu)
-        update(xd)
+            rso[l, 1, k] = (gs[l, k, xd, 1].astype(F32) + rst[l, 1, k].astype(F32)).astype(BF16)
+            scatter_copy(rso.at[l, 1, k], rsb.at[l, 1, k, 1], 5, k, down)
+
+        update(1)
+        scatter_far(1)
+        scatter_plain(1)
+        update(0)
+        scatter_far(0)
+        scatter_sum(1)
         scatter_plain(0)
         scatter_sum(0)
-        scatter_plain(1)
-        scatter_sum(1)
-        update(x)
         if l == 0:
             ring_forward(1, 0, 0)
             ring_forward(1, 0, 1)
         drain_upto = len(sends)
-        for k in range(2):
-            arrive(rsb.at[l, 0, 2 + k], rs_r.at[l, 2, k])
-            arrive(rsb.at[l, 1, k], rs_r.at[l, 3, k])
-            arrive(rsb.at[l, 0, k], rs_r.at[l, 4, k])
-            arrive(rsb.at[l, 1, 2 + k], rs_r.at[l, 5, k])
-            for q in (k, 2 + k):
-                total = gs[l, x, q].astype(F32) + rsb[l, 0, q].astype(F32) + rsb[l, 1, q].astype(F32)
-                resid[quarter(q)] += total
+        for k in (1, 0):
+            arrive(rsb.at[l, 0, k, 1], rs_r.at[l, 2, k])
+            arrive(rsb.at[l, 1, k, 0], rs_r.at[l, 3, k])
+            arrive(rsb.at[l, 0, k, 0], rs_r.at[l, 4, k])
+            arrive(rsb.at[l, 1, k, 1], rs_r.at[l, 5, k])
+            for e in range(2):
+                total = gs[l, k, x, e].astype(F32) + rsb[l, 0, k, e].astype(F32) + rsb[l, 1, k, e].astype(F32)
+                resid[slot(k, e)] += total
                 if l == 0:
-                    norm_rows(1, q)
+                    norm_rows(1, k, e)
             if l == 0:
                 gather_send(1, k)
             else:
                 finish(k)
         if l == 0:
-            gather_forward(1, 0)
+            gather_forward(1, 1)
             ring_forward(1, 0, 2)
             ring_forward(1, 0, 3)
-            gather_forward(1, 1)
+            gather_forward(1, 0)
+            gather_sides(1, 1)
             ring_send(1, 1)
-            gather_sides(1)
             for copy in sends[:drain_upto]:
                 copy.wait_send()
             del sends[:drain_upto]
-            gather_far(1)
+            gather_far(1, 1)
             ring_end(1, 0)
 
     for p in range(4):
@@ -466,6 +487,8 @@
 
     for copy, here in last:
         settle(copy, jnp.logical_not(here))
+    for par in range(2):
+        settle(latent_pass(0, par), c != y // 2)
     for copy, t in scattered:
         settle(copy, t != x)
     for copy in sends:
@@ -493,7 +516,7 @@
             vmem((16, 16, QP), BF16),
             vmem((16, 16, QP), BF16),
             vmem((8, 2, 16, QP), BF16),
-            vmem((2, 2, 4, 16, QP), BF16),
+            vmem((2, 2, 2, 2, 16, QP), BF16),
             vmem((LAYERS, 16, 2, 16, QP), BF16),
             vmem((LAYERS, 4, 4, 8, 16, QP), BF16),
             vmem((LAYERS, 4, 4, 8, 16, 128), BF16),
@@ -501,20 +524,20 @@
             vmem((LAYERS, 2, 4, 4, 16, DP), BF16),
             vmem((2, 256, 384), BF16),
             vmem((LAYERS, 256, 256), BF16),
-            vmem((2, 4, 64, 128), BF16),
-            vmem((LAYERS, 4, 64, 128), BF16),
-            vmem((LAYERS, 4, 4, 16, DP), BF16),
-            vmem((LAYERS, 2, 4, 16, DP), BF16),
+            vmem((2, 4, 4, 16, 128), BF16),
+            vmem((LAYERS, 2, 4, 2, 16, 128), BF16),
+            vmem((LAYERS, 2, 4, 2, 16, DP), BF16),
+            vmem((LAYERS, 2, 2, 2, 16, DP), BF16),
             vmem((LAYERS, 2, 2, 16, DP), BF16),
             vmem((LAYERS, 2, 2, 16, DP), BF16),
-            vmem((4, 16, D), BF16),
+            vmem((2, 2, 16, D), BF16),
             vmem((D // 128, 384, 128), BF16),
-            dma((16,)), dma((16,)), dma((8,)), dma((8,)),
+            dma((16,)), dma((16,)), dma((4, 2)), dma((2, 2, 2)),
             dma((LAYERS, 2, 8)), dma((LAYERS, 2, 8)), dma((LAYERS, 16, 2)), dma((LAYERS, 4)),
             dma((LAYERS, 2, 2, 4)), dma((LAYERS, 2, 2, 4)), dma((LAYERS, 2, 4)), dma((LAYERS, 2, 4)),
-            dma((LAYERS,)), dma((LAYERS,)), dma((LAYERS, 11, 2)), dma((LAYERS, 11, 2)),
-            dma((LAYERS,)), dma((LAYERS,)), dma((LAYERS,)), dma((LAYERS,)),
-            dma((LAYERS, 6, 2)), dma((LAYERS, 6, 2)), dma((4,)), dma((4,)),
+            dma((LAYERS,)), dma((LAYERS,)), dma((LAYERS, 10, 2)), dma((LAYERS, 10, 2)),
+            dma((LAYERS,)), dma((LAYERS,)), dma((LAYERS, 2)), dma((LAYERS, 2)),
+            dma((LAYERS, 6, 2)), dma((LAYERS, 6, 2)), dma((2, 2)), dma((4,)),
         ],
         compiler_params=pltpu.CompilerParams(
             collective_id=0, has_side_effects=True, vmem_limit_bytes=56 * 2**20

time: 140 us -> 138 us (0.986)
  Pallas kernels: 136 us -> 134 us
    pallas_call x1, Pallas kernels: 136 us -> 134 us  [local(): pl.pallas_call(kernel, out_shape=jax.ShapeDtypeStruct((4, 16, D), BF16),...]
where the time goes in v5:
time: 138 us
  Pallas kernels  134 us (97%)
  local copies, waits for them, and re-layouts  3.32 us (2%)
    pallas_call x1, Pallas kernels, local(): pl.pallas_call(kernel, out_shape=jax.ShapeDtypeStruct((4, 16, D), BF16),...  134 us

profile of v5, /device:TPU:5, one launch (start us, length us, event | category | flops | bytes accessed | tf_op | source)
XLA Modules:
  0.0 137.8 jit_solution(1248268922014282865)
XLA Ops:
  0.0 0.0 copy-start
  0.7 0.8 concatenate.9
  1.4 0.0 copy-done
  1.5 0.1 concatenate.8
  1.6 0.1 maximum_bitcast_fusion
  1.7 0.6 pad.4.wloc_ref
  2.4 133.7 %shard_map.55 = bf16[4,16,1920]{2,1,0:T(8,128)(2,1)} custom-call(bf16[480,256]{1,0:T(8,128)(2,1)} %bitcast.12, s32[1]{0:T(128)S(6)} %copy.11.start_ref, f32[2,1920]{1,0:T(2,128)} %gain_ref.1, bf16[2,2,16,512]{3,2,1,0:T(8,128)(2,1)} %pad.4.wloc_ref), custom_call_target="tpu_custom_call" | custom-call | tf_op jit(solution)/shard_map/pallas_call | solution.py:504
  136.1 1.7 %reshape.11 = bf16[32,2,1920]{2,1,0:T(2,128)(2,1)} reshape(bf16[4,16,1920]{2,1,0:T(8,128)(2,1)} %shard_map.55) | data formatting | bytes 491520 | tf_op jit(solution)/shard_map/reshape | solution.py:546
  (4 shorter events, 0.1 us)
Async XLA Ops:
  0.0 1.5 %copy-start = (bf16[2,15,3,256]{3,0,2,1:T(2,128)(2,1)S(1)}, bf16[2,15,3,256]{3,0,2,1:T(2,128)(2,1)}, u32[]{:S(2)}) copy-start(bf16[2,15,3,256]{3,0,2,1:T(2,128)(2,1)} %param.8) | copy-start | bytes 138244

commit v6 on v5

--- a/solution.py
+++ b/solution.py
@@ -142,21 +142,20 @@
         return wf.at[l, yy, xx, :, :, pl.ds(0, 384) if part == 0 else pl.ds(384, 128)]
 
     def ring_send(l, part):
-        for p in range(4):
-            if part == 0:
-                arrive(piece(l, y, p), wx_r.at[l, p])
-            block = lanes(l, y, p, part)
-            for d, to in ((0, yu), (1, yd)):
+        for n in range(4):
+            if part == 0 and n < 2:
+                for p in (n, n + 2):
+                    arrive(piece(l, y, p), wx_r.at[l, p])
+            for d, to, p in ((0, yu, n), (1, yd, (n + 2) % 4)):
+                block = lanes(l, y, p, part)
                 send(block, block, wy_s.at[l, part, d, p], wy_r.at[l, part, d, p], dev(x, to, z, c))
 
-    def ring_forward(l, part, p):
-        below, above = lanes(l, yd, p, part), lanes(l, yu, p, part)
-        arrive(below, wy_r.at[l, part, 0, p])
-        if p < 2:
-            send(below, below, wg_s.at[l, part, p], wg_r.at[l, part, p], dev(x, yu, z, c))
-        arrive(above, wy_r.at[l, part, 1, p])
-        if p >= 2:
-            send(above, above, wg_s.at[l, part, p], wg_r.at[l, part, p], dev(x, yd, z, c))
+    def ring_forward(l, part, n):
+        for d, yy, to, p in ((0, yd, yu, n), (1, yu, yd, (n + 2) % 4)):
+            block = lanes(l, yy, p, part)
+            arrive(block, wy_r.at[l, part, d, p])
+            if n < 2:
+                send(block, block, wg_s.at[l, part, p], wg_r.at[l, part, p], dev(x, to, z, c))
 
     def ring_end(l, part):
         for p in range(4):

time: 138 us -> 135 us (0.978)
  Pallas kernels: 134 us -> 131 us
    pallas_call x1, Pallas kernels: 134 us -> 131 us  [local(): pl.pallas_call(kernel, out_shape=jax.ShapeDtypeStruct((4, 16, D), BF16),...]
where the time goes in v6:
time: 135 us
  Pallas kernels  131 us (97%)
  local copies, waits for them, and re-layouts  3.32 us (2%)
    pallas_call x1, Pallas kernels, local(): pl.pallas_call(kernel, out_shape=jax.ShapeDtypeStruct((4, 16, D), BF16),...  131 us

profile of v6, /device:TPU:5, one launch (start us, length us, event | category | flops | bytes accessed | tf_op | source)
XLA Modules:
  0.0 135.2 jit_solution(17684825684532710176)
XLA Ops:
  0.0 0.0 copy-start
  0.7 0.8 concatenate.9
  1.4 0.0 copy-done
  1.5 0.1 concatenate.8
  1.6 0.1 maximum_bitcast_fusion
  1.7 0.6 pad.4.wloc_ref
  2.4 131.1 %shard_map.55 = bf16[4,16,1920]{2,1,0:T(8,128)(2,1)} custom-call(bf16[480,256]{1,0:T(8,128)(2,1)} %bitcast.12, s32[1]{0:T(128)S(6)} %copy.11.start_ref, f32[2,1920]{1,0:T(2,128)} %gain_ref.1, bf16[2,2,16,512]{3,2,1,0:T(8,128)(2,1)} %pad.4.wloc_ref), custom_call_target="tpu_custom_call" | custom-call | tf_op jit(solution)/shard_map/pallas_call | solution.py:503
  133.5 1.7 %reshape.11 = bf16[32,2,1920]{2,1,0:T(2,128)(2,1)} reshape(bf16[4,16,1920]{2,1,0:T(8,128)(2,1)} %shard_map.55) | data formatting | bytes 491520 | tf_op jit(solution)/shard_map/reshape | solution.py:545
  (4 shorter events, 0.1 us)
Async XLA Ops:
  0.0 1.5 %copy-start = (bf16[2,15,3,256]{3,0,2,1:T(2,128)(2,1)S(1)}, bf16[2,15,3,256]{3,0,2,1:T(2,128)(2,1)}, u32[]{:S(2)}) copy-start(bf16[2,15,3,256]{3,0,2,1:T(2,128)(2,1)} %param.8) | copy-start | bytes 138244
